TPU v7x, 32 devices: a whole 2x2x4 slice. The times are simulated.
32 devices in a mesh: ctx: 4 (over z), head: 4 (over x, core), band: 2 (over y).
Axes of the slice: x: 2, y: 2, z: 4, core: 2. Of those that a mesh axis runs over, the one named last changes fastest.
Arguments:
- queries: bfloat16 [8192, 1024], P(('band', 'ctx', 'head')), parts along dimension 0, may hold values from -6 to 6
- key_states: bfloat16 [8192, 1024], P(('band', 'ctx', 'head')), parts along dimension 0, may hold values from -6 to 6
- value_states: bfloat16 [8192, 1024], P(('band', 'ctx', 'head')), parts along dimension 0, may hold values from -6 to 6
- grad_output: bfloat16 [8192, 1024], P(('band', 'ctx', 'head')), parts along dimension 0, may hold values from -24 to 24
- block_slot: int32 [128], P('band'), parts along dimension 0, may hold values from 0 to 63, as said below
- neighbours: int32 [128, 8], P('band'), parts along dimension 0, may hold values from 0 to 63, as said below
Outputs:
- grad_queries: bfloat16 [8192, 1024], P(('band', 'ctx', 'head')), parts along dimension 0
- grad_keys: bfloat16 [8192, 1024], P(('band', 'ctx', 'head')), parts along dimension 0
- grad_values: bfloat16 [8192, 1024], P(('band', 'ctx', 'head')), parts along dimension 0
There are 2 independent parts, one for each index of `band`. A program takes and returns all parts, laid end to end along the dimension named above; each array names one. Nothing has to cross between parts.
Inputs may be any that keep to these rules, and one draw needn't show every extreme that they name: `block_slot`: a permutation of the 64 slots. `neighbours`: entry 0 of row b is b. The slot of every other entry lies on a ctx index, slot // 16, at most 1 away cyclically from that of b. These entries are distinct where at least 7 such blocks exist, and else repeat.
All inputs are finite; a program needn't handle non-finite values.
Results may differ from a plain program's by a relative error of at most 0.0088.
Values may be sent and summed in bfloat16 or wider, within the bound.
No kernel may reach another device: no remote copies, remote signals or barrier semaphores. Data moves between devices by JAX's collectives and lax.ppermute only.
A program may use at most 128 MiB of HBM per device.

v0:
```python
import math

import jax
import jax.numpy as jnp
from jax import lax
from jax.sharding import PartitionSpec as P

HEAD_DIM = 64
BLOCK_TOK = 64
NBR = 8
REACH = 1


def from_behind(value, axis, steps):
    count = lax.axis_size(axis)
    pairs = [(source, (source + steps) % count) for source in range(count)]
    return lax.ppermute(value, axis, pairs)


def body(queries, key_states, value_states, grad_output, block_slot, neighbours):
    query_loc, key_loc, value_loc, grad_loc = (
        lax.all_to_all(queries, "head", split_axis=1, concat_axis=0, tiled=True),
        lax.all_to_all(key_states, "head", split_axis=1, concat_axis=0, tiled=True),
        lax.all_to_all(value_states, "head", split_axis=1, concat_axis=0, tiled=True),
        lax.all_to_all(grad_output, "head", split_axis=1, concat_axis=0, tiled=True),
    )
    row_count, feat_count = query_loc.shape
    block_count = row_count // BLOCK_TOK
    head_count = feat_count // HEAD_DIM
    ctx_size = lax.axis_size("ctx")
    ctx_here = lax.axis_index("ctx")
    slot_count = block_slot.shape[0]
    slot_ids = jnp.arange(slot_count, dtype=jnp.int32)
    matches = (block_slot[None, :] == slot_ids[:, None]).astype(jnp.int32)
    sphere_of = jnp.sum(matches * slot_ids[None, :], axis=1)
    my_slots = ctx_here * block_count + jnp.arange(block_count, dtype=jnp.int32)
    listed = block_slot[neighbours[sphere_of[my_slots]]]
    key_value = jnp.stack((key_loc, value_loc))
    pieces = []
    for offset in range(-REACH, REACH + 1):
        if offset == 0:
            pieces.append(key_value)
        else:
            pieces.append(from_behind(key_value, "ctx", -offset))
    gathered = jnp.concatenate(pieces, axis=1)
    owner_gap = (listed // block_count - ctx_here + ctx_size + REACH) % ctx_size - REACH
    lookup = (owner_gap + REACH) * block_count + listed % block_count
    span_blocks = gathered.shape[1] // BLOCK_TOK
    kv_table = gathered.reshape(2, span_blocks, BLOCK_TOK, feat_count)
    query_blocks = query_loc.reshape(block_count, BLOCK_TOK, head_count, HEAD_DIM)
    grad_blocks = grad_loc.reshape(block_count, BLOCK_TOK, head_count, HEAD_DIM)
    softmax_scale = HEAD_DIM ** (-0.5)
    group = math.gcd(block_count, max(1, 512 // BLOCK_TOK))
    group_count = block_count // group

    def one_group(group_id):
        first = group_id * group
        chosen = lax.dynamic_slice_in_dim(lookup, first, group, 0)
        keyval_now = kv_table[:, chosen].reshape(2, group, NBR * BLOCK_TOK, head_count, HEAD_DIM)
        key_rows = keyval_now[0]
        value_rows = keyval_now[1]
        query_rows = lax.dynamic_slice_in_dim(query_blocks, first, group, 0)
        grad_rows = lax.dynamic_slice_in_dim(grad_blocks, first, group, 0)
        scores = (
            jnp.einsum("gqhd,gkhd->ghqk", query_rows, key_rows, preferred_element_type=jnp.float32)
            * softmax_scale
        )
        row_max = jnp.max(scores, axis=3, keepdims=True)
        weights = jnp.exp(scores - row_max)
        probability = weights / jnp.sum(weights, axis=3, keepdims=True)
        grad_prob = jnp.einsum(
            "gqhd,gkhd->ghqk", grad_rows, value_rows, preferred_element_type=jnp.float32
        )
        row_delta = jnp.sum(probability * grad_prob, axis=3, keepdims=True)
        score_low = (probability * (grad_prob - row_delta)).astype(jnp.bfloat16)
        prob_low = probability.astype(jnp.bfloat16)
        grad_value = jnp.einsum(
            "ghqk,gqhd->gkhd", prob_low, grad_rows, preferred_element_type=jnp.float32
        )
        grad_key = (
            jnp.einsum("ghqk,gqhd->gkhd", score_low, query_rows, preferred_element_type=jnp.float32)
            * softmax_scale
        )
        grad_query = (
            jnp.einsum("ghqk,gkhd->gqhd", score_low, key_rows, preferred_element_type=jnp.float32)
            * softmax_scale
        )
        both = jnp.stack(
            (
                grad_key.reshape(group, NBR, BLOCK_TOK, feat_count),
                grad_value.reshape(group, NBR, BLOCK_TOK, feat_count),
            ),
            axis=2,
        )
        return (
            grad_query.astype(jnp.bfloat16),
            both.reshape(group * NBR, 2 * BLOCK_TOK * feat_count),
        )

    query_parts, contributions = lax.map(one_group, jnp.arange(group_count, dtype=jnp.int32))
    contributions = contributions.reshape(block_count * NBR, 2 * BLOCK_TOK * feat_count)
    selector = (
        lookup.reshape(-1)[None, :] == jnp.arange(span_blocks, dtype=jnp.int32)[:, None]
    ).astype(jnp.float32)
    grad_flat = jnp.dot(
        selector, contributions, precision=lax.Precision.HIGHEST, preferred_element_type=jnp.float32
    )
    returned = grad_flat.reshape(2 * REACH + 1, block_count, 2, BLOCK_TOK, feat_count)
    summed = returned[REACH]
    for offset in range(-REACH, REACH + 1):
        if offset != 0:
            summed = summed + from_behind(returned[offset + REACH], "ctx", offset)
    grad_keyval = summed.astype(jnp.bfloat16)
    key_rows_out = grad_keyval[:, 0].reshape(row_count, feat_count)
    value_rows_out = grad_keyval[:, 1].reshape(row_count, feat_count)
    query_rows_out = query_parts.reshape(row_count, feat_count)
    out_query, out_key, out_value = (
        lax.all_to_all(query_rows_out, "head", split_axis=0, concat_axis=1, tiled=True),
        lax.all_to_all(key_rows_out, "head", split_axis=0, concat_axis=1, tiled=True),
        lax.all_to_all(value_rows_out, "head", split_axis=0, concat_axis=1, tiled=True),
    )
    return (out_query, out_key, out_value)


def solution(mesh):
    in_specs = (
        P(("band", "ctx", "head"), None),
        P(("band", "ctx", "head"), None),
        P(("band", "ctx", "head"), None),
        P(("band", "ctx", "head"), None),
        P("band"),
        P("band", None),
    )
    out_specs = (
        P(("band", "ctx", "head"), None),
        P(("band", "ctx", "head"), None),
        P(("band", "ctx", "head"), None),
    )
    return jax.shard_map(body, mesh=mesh, in_specs=in_specs, out_specs=out_specs, check_vma=False)
```

profile of v0, /device:TPU:1, one launch (start us, length us, event | category | flops | bytes accessed | tf_op | source)
XLA Modules:
  0.0 437.3 jit_solution(15421186414857736438)
XLA Ops:
  21.4 6.1 %all-to-all-done.1 = bf16[256,4,256]{2,0,1:T(8,128)(2,1)S(1)} async-done(((bf16[256,4,256]{2,0,1:T(8,128)(2,1)}), bf16[256,4,256]{2,0,1:T(8,128)(2,1)S(1)}, u32[]{:S(2)}, u32[]{:S(2)}) %all-to-all-start.1) | async-done | bytes 524320 | tf_op jit(solution)/shard_map/all_to_all | solution.py:24
  58.6 23.4 %collective-permute-done = bf16[2,1024,256]{2,1,0:T(8,128)(2,1)} collective-permute-done((bf16[2,1024,256]{2,1,0:T(8,128)(2,1)S(1)}, bf16[2,1024,256]{2,1,0:T(8,128)(2,1)}, u32[]{:S(2)}, u32[]{:S(2)}) %collective-permute-start) | collective-permute-done | bytes 1048608 | tf_op jit(solution)/shard_map/ppermute | solution.py:17
  84.1 217.0 %while.12 = (s32[]{:T(128)}, bf16[2,8,64,4,64]{2,1,0,4,3:T(8,128)(2,1)}, f32[2,64,32768]{2,1,0:T(8,128)}, s32[2]{0:T(128)S(1)}, s32[16,8]{1,0:T(8,128)S(1)}, /*i...) while((s32[]{:T(128)}, ...), condition=%wide.region_5.6_spmd, body=%wide.region_1.5_spmd.sunk | while | flops 687079104 | bytes 216323984 | solution.py:100
  95.2 9.1 %copy.133 = bf16[8,8,2,64,256]{3,1,4,0,2:T(8,128)(2,1)} copy(bf16[8,8,2,64,256]{4,3,2,1,0:T(8,128)(2,1)} %bitcast.124) | data formatting | bytes 8388608 | tf_op jit(solution)/shard_map/while/body/eval_jaxpr/gather | solution.py:59
  115.5 6.5 %squeeze.23 = bf16[8,512,4,64]{1,3,2,0:T(8,128)(2,1)} reshape(bf16[1,8,8,64,256]{3,2,4,1,0:T(8,128)(2,1)} %get-tuple-element.191) | data formatting | bytes 4194304 | tf_op jit(solution)/shard_map/while/body/eval_jaxpr/squeeze | solution.py:61
  137.7 7.1 %reshape.228 = f32[8,8,1,64,256]{3,1,4,0,2:T(8,128)} reshape(f32[8,512,4,64]{1,3,2,0:T(8,128)} %multiply_bitcast_fusion.2) | data formatting | bytes 8388608 | tf_op jit(solution)/shard_map/while/body/eval_jaxpr/stack;while/body/eval_jaxpr/reshape | solution.py:88
  144.8 7.1 %reshape.227 = f32[8,8,1,64,256]{3,1,4,0,2:T(8,128)} reshape(f32[8,512,4,64]{1,3,2,0:T(8,128)} %convolution_bitcast_fusion.2) | data formatting | bytes 8388608 | tf_op jit(solution)/shard_map/while/body/eval_jaxpr/stack;while/body/eval_jaxpr/reshape | solution.py:88
  151.8 11.3 %pad_maximum_fusion.4 = f32[8,8,2,64,256]{3,1,4,0,2:T(8,128)} fusion(f32[8,8,1,64,256]{3,1,4,0,2:T(8,128)} %reshape.227, f32[8,8,1,64,256]{3,1,4,0,2:T(8,128)} %reshape.228), kind=kLoop, calls=%fused_computation.5.clone.1 | loop fusion | flops 2097152 | bytes 16777216 | tf_op jit(solution)/shard_map/while/body/eval_jaxpr/stack | solution.py:88
  163.1 12.8 %copy.136 = f32[8,8,2,64,256]{4,3,2,1,0:T(8,128)} copy(f32[8,8,2,64,256]{3,1,4,0,2:T(8,128)} %pad_maximum_fusion.4) | data formatting | bytes 16777216 | tf_op jit(solution)/shard_map/while/body/eval_jaxpr/stack | solution.py:88
  175.9 9.4 %broadcast_in_dim.30 = f32[1,64,32768]{2,1,0:T(8,128)} reshape(f32[8,8,2,64,256]{4,3,2,1,0:T(8,128)} %copy.136) | data formatting | bytes 16777216 | tf_op jit(solution)/shard_map/while/body/jit(dynamic_update_index_in_dim)/broadcast_in_dim | solution.py:100
  185.4 7.4 %constant_dynamic-update-slice_fusion.2 = f32[2,64,32768]{2,1,0:T(8,128)} fusion(f32[2,64,32768]{2,1,0:T(8,128)} %get-tuple-element.208, f32[1,64,32768]{2,1,0:T(8,128)} %broadcast_in_dim.30, s32[]{:T(128)S(6)} %copy.142), kind=kLoop, calls=%fused_computation.25.clone.1 | loop fusion | bytes 16777220 | tf_op jit(solution)/shard_map/while/body/jit(dynamic_update_index_in_dim)/dynamic_update_slice | solution.py:100
  203.6 9.1 %copy.133 = bf16[8,8,2,64,256]{3,1,4,0,2:T(8,128)(2,1)} copy(bf16[8,8,2,64,256]{4,3,2,1,0:T(8,128)(2,1)} %bitcast.124) | data formatting | bytes 8388608 | tf_op jit(solution)/shard_map/while/body/eval_jaxpr/gather | solution.py:59
  223.9 6.5 %squeeze.23 = bf16[8,512,4,64]{1,3,2,0:T(8,128)(2,1)} reshape(bf16[1,8,8,64,256]{3,2,4,1,0:T(8,128)(2,1)} %get-tuple-element.191) | data formatting | bytes 4194304 | tf_op jit(solution)/shard_map/while/body/eval_jaxpr/squeeze | solution.py:61
  246.1 7.1 %reshape.228 = f32[8,8,1,64,256]{3,1,4,0,2:T(8,128)} reshape(f32[8,512,4,64]{1,3,2,0:T(8,128)} %multiply_bitcast_fusion.2) | data formatting | bytes 8388608 | tf_op jit(solution)/shard_map/while/body/eval_jaxpr/stack;while/body/eval_jaxpr/reshape | solution.py:88
  253.2 7.1 %reshape.227 = f32[8,8,1,64,256]{3,1,4,0,2:T(8,128)} reshape(f32[8,512,4,64]{1,3,2,0:T(8,128)} %convolution_bitcast_fusion.2) | data formatting | bytes 8388608 | tf_op jit(solution)/shard_map/while/body/eval_jaxpr/stack;while/body/eval_jaxpr/reshape | solution.py:88
  260.2 11.3 %pad_maximum_fusion.4 = f32[8,8,2,64,256]{3,1,4,0,2:T(8,128)} fusion(f32[8,8,1,64,256]{3,1,4,0,2:T(8,128)} %reshape.227, f32[8,8,1,64,256]{3,1,4,0,2:T(8,128)} %reshape.228), kind=kLoop, calls=%fused_computation.5.clone.1 | loop fusion | flops 2097152 | bytes 16777216 | tf_op jit(solution)/shard_map/while/body/eval_jaxpr/stack | solution.py:88
  271.5 12.8 %copy.136 = f32[8,8,2,64,256]{4,3,2,1,0:T(8,128)} copy(f32[8,8,2,64,256]{3,1,4,0,2:T(8,128)} %pad_maximum_fusion.4) | data formatting | bytes 16777216 | tf_op jit(solution)/shard_map/while/body/eval_jaxpr/stack | solution.py:88
  284.3 9.4 %broadcast_in_dim.30 = f32[1,64,32768]{2,1,0:T(8,128)} reshape(f32[8,8,2,64,256]{4,3,2,1,0:T(8,128)} %copy.136) | data formatting | bytes 16777216 | tf_op jit(solution)/shard_map/while/body/jit(dynamic_update_index_in_dim)/broadcast_in_dim | solution.py:100
  293.8 7.4 %constant_dynamic-update-slice_fusion.2 = f32[2,64,32768]{2,1,0:T(8,128)} fusion(f32[2,64,32768]{2,1,0:T(8,128)} %get-tuple-element.208, f32[1,64,32768]{2,1,0:T(8,128)} %broadcast_in_dim.30, s32[]{:T(128)S(6)} %copy.142), kind=kLoop, calls=%fused_computation.25.clone.1 | loop fusion | bytes 16777220 | tf_op jit(solution)/shard_map/while/body/jit(dynamic_update_index_in_dim)/dynamic_update_slice | solution.py:100
  301.1 9.6 %fusion.11 = f32[48,32768]{1,0:T(8,128)S(1)} fusion(f32[128,32768]{1,0:T(8,128)} %bitcast.126, s32[128]{0:T(128)S(1)} %copy-done.13), kind=kOutput, calls=%fused_computation.33 | convolution fusion | flops 2415925248 | bytes 23069184 | tf_op jit(solution)/shard_map/dot_general | solution.py:105
  326.8 36.9 %collective-permute-done.3 = f32[16,2,64,256]{3,2,1,0:T(8,128)} collective-permute-done((f32[16,2,64,256]{3,2,1,0:T(8,128)}, f32[16,2,64,256]{3,2,1,0:T(8,128)}, u32[]{:S(2)}, u32[]{:S(2)}) %collective-permute-start.3) | collective-permute-done | bytes 2097184 | tf_op jit(solution)/shard_map/ppermute | solution.py:17
  363.7 45.1 %collective-permute-done.2 = f32[16,2,64,256]{3,2,1,0:T(8,128)} collective-permute-done((f32[16,2,64,256]{3,2,1,0:T(8,128)}, f32[16,2,64,256]{3,2,1,0:T(8,128)}, u32[]{:S(2)}, u32[]{:S(2)}) %collective-permute-start.2) | collective-permute-done | bytes 2097184 | tf_op jit(solution)/shard_map/ppermute | solution.py:17
  412.4 11.2 %all_to_all.121 = bf16[4,256,256]{2,1,0:T(8,128)(2,1)S(1)} all-to-all(bf16[4,256,256]{2,1,0:T(8,128)(2,1)S(1)} %bitcast.142), channel_id=1, replica_groups=mesh['ctx'=4,'head'=4,'band'=2] {'head'}, dimensions={0} | all-to-all | bytes 1048576 | tf_op jit(solution)/shard_map/all_to_all | solution.py:119
  430.4 5.8 %all-to-all-done.6 = bf16[4,256,256]{2,1,0:T(8,128)(2,1)S(1)} async-done(((bf16[4,256,256]{2,1,0:T(8,128)(2,1)}), bf16[4,256,256]{2,1,0:T(8,128)(2,1)S(1)}, u32[]{:S(2)}, u32[]{:S(2)}) %all-to-all-start.6) | async-done | bytes 524320 | tf_op jit(solution)/shard_map/all_to_all | solution.py:120
  (136 shorter events, 155.2 us)
Async XLA Ops:
  0.6 18.9 %copy-start.12 = (s32[64,8]{0,1:T(8,128)S(1)}, s32[64,8]{0,1:T(8,128)}, u32[]{:S(2)}) copy-start(s32[64,8]{0,1:T(8,128)} %param.13) | copy-start | bytes 6148
  0.6 19.0 %copy-start.10 = (bf16[256,1024]{1,0:T(8,128)(2,1)S(1)}, bf16[256,1024]{1,0:T(8,128)(2,1)}, u32[]{:S(2)}) copy-start(bf16[256,1024]{1,0:T(8,128)(2,1)} %param.8) | copy-start | bytes 1572868
  0.7 20.0 %copy-start = (s32[64]{0:T(128)S(1)}, s32[64]{0:T(128)}, u32[]{:S(2)}) copy-start(s32[64]{0:T(128)} %param.12) | copy-start | bytes 772
  3.0 12.1 %all-to-all-start = ((bf16[256,4,256]{2,0,1:T(8,128)(2,1)}), bf16[256,4,256]{2,0,1:T(8,128)(2,1)S(1)}, u32[]{:S(2)}, u32[]{:S(2)}) async-start(bf16[256,4,256]{2,0,1:T(8,128)(2,1)} %copy.101), calls=%async_computation | async-start | bytes 1048576 | tf_op jit(solution)/shard_map/all_to_all | solution.py:23
  15.0 23.0 %copy-start.6 = (bf16[256,4,256]{2,0,1:T(8,128)(2,1)}, bf16[256,4,256]{2,0,1:T(8,128)(2,1)S(1)}, u32[]{:S(2)}) copy-start(bf16[256,4,256]{2,0,1:T(8,128)(2,1)S(1)} %all-to-all-done) | copy-start | bytes 1572868
  15.0 12.5 %all-to-all-start.1 = ((bf16[256,4,256]{2,0,1:T(8,128)(2,1)}), bf16[256,4,256]{2,0,1:T(8,128)(2,1)S(1)}, u32[]{:S(2)}, u32[]{:S(2)}) async-start(bf16[256,4,256]{2,0,1:T(8,128)(2,1)} %copy.103), calls=%async_computation.1 | async-start | bytes 1048576 | tf_op jit(solution)/shard_map/all_to_all | solution.py:24
  27.5 10.6 %copy-start.7 = (bf16[256,4,256]{2,0,1:T(8,128)(2,1)}, bf16[256,4,256]{2,0,1:T(8,128)(2,1)S(1)}, u32[]{:S(2)}) copy-start(bf16[256,4,256]{2,0,1:T(8,128)(2,1)S(1)} %all-to-all-done.1) | copy-start | bytes 1572868
  27.5 12.4 %all-to-all-start.2 = ((bf16[256,4,256]{0,2,1:T(8,128)(2,1)}), bf16[256,4,256]{0,2,1:T(8,128)(2,1)S(1)}, u32[]{:S(2)}, u32[]{:S(2)}) async-start(bf16[256,4,256]{0,2,1:T(8,128)(2,1)} %bitcast.18), calls=%async_computation.2 | async-start | bytes 1048576 | tf_op jit(solution)/shard_map/all_to_all | solution.py:22
  31.9 26.6 %collective-permute-start.1 = (bf16[2,1024,256]{2,1,0:T(8,128)(2,1)S(1)}, bf16[2,1024,256]{2,1,0:T(8,128)(2,1)}, u32[]{:S(2)}, u32[]{:S(2)}) collective-permute-start(bf16[2,1024,256]{2,1,0:T(8,128)(2,1)S(1)} %pad_maximum_fusion.2), channel_id=1, source_target_pairs={{0,24},{8,0},{16,8},{24,16},{1,25},{9,1},{17,9},{25,17},{2,26},{10... | collective-permute-start | bytes 3145736 | tf_op jit(solution)/shard_map/ppermute | solution.py:17
  36.0 46.0 %collective-permute-start = (bf16[2,1024,256]{2,1,0:T(8,128)(2,1)S(1)}, bf16[2,1024,256]{2,1,0:T(8,128)(2,1)}, u32[]{:S(2)}, u32[]{:S(2)}) collective-permute-start(bf16[2,1024,256]{2,1,0:T(8,128)(2,1)S(1)} %pad_maximum_fusion.2), channel_id=1, source_target_pairs={{0,8},{8,16},{16,24},{24,0},{1,9},{9,17},{17,25},{25,1},{2,10},{10... | collective-permute-start | bytes 3145736 | tf_op jit(solution)/shard_map/ppermute | solution.py:17
  39.9 12.3 %all-to-all-start.3 = ((bf16[256,4,256]{0,2,1:T(8,128)(2,1)}), bf16[256,4,256]{0,2,1:T(8,128)(2,1)S(1)}, u32[]{:S(2)}, u32[]{:S(2)}) async-start(bf16[256,4,256]{0,2,1:T(8,128)(2,1)} %bitcast.20), calls=%async_computation.3 | async-start | bytes 1048576 | tf_op jit(solution)/shard_map/all_to_all | solution.py:25
  84.1 217.0 %copy-start.13 = (s32[128]{0:T(128)S(1)}, s32[128]{0:T(128)}, u32[]{:S(2)}) copy-start(s32[128]{0:T(128)} %fusion.19) | copy-start | bytes 1540
  84.3 10.9 %copy-start.2 = (bf16[2,48,64,256]{3,2,1,0:T(8,128)(2,1)}, bf16[2,48,64,256]{3,2,1,0:T(8,128)(2,1)S(1)}, u32[]{:S(2)}) copy-start(bf16[2,48,64,256]{3,2,1,0:T(8,128)(2,1)S(1)} %get-tuple-element.223) | copy-start | bytes 9437188 | tf_op jit(solution)/shard_map/while
  115.5 6.5 %copy-start.4 = (bf16[8,64,4,64]{3,1,2,0:T(8,128)(2,1)S(1)}, bf16[8,64,4,64]{3,1,2,0:T(8,128)(2,1)}, u32[]{:S(2)}) copy-start(bf16[8,64,4,64]{3,1,2,0:T(8,128)(2,1)} %copy.134) | copy-start | bytes 786436 | tf_op jit(solution)/shard_map/while
  125.2 4.0 copy-start.1
  185.4 7.4 %copy-start.3 = (bf16[2,48,64,256]{3,2,1,0:T(8,128)(2,1)S(1)}, bf16[2,48,64,256]{3,2,1,0:T(8,128)(2,1)}, u32[]{:S(2)}) copy-start(bf16[2,48,64,256]{3,2,1,0:T(8,128)(2,1)} %copy-done.2) | copy-start | bytes 9437188 | tf_op jit(solution)/shard_map/while
  192.8 10.8 %copy-start.2 = (bf16[2,48,64,256]{3,2,1,0:T(8,128)(2,1)}, bf16[2,48,64,256]{3,2,1,0:T(8,128)(2,1)S(1)}, u32[]{:S(2)}) copy-start(bf16[2,48,64,256]{3,2,1,0:T(8,128)(2,1)S(1)} %get-tuple-element.223) | copy-start | bytes 9437188 | tf_op jit(solution)/shard_map/while
  223.9 6.5 %copy-start.4 = (bf16[8,64,4,64]{3,1,2,0:T(8,128)(2,1)S(1)}, bf16[8,64,4,64]{3,1,2,0:T(8,128)(2,1)}, u32[]{:S(2)}) copy-start(bf16[8,64,4,64]{3,1,2,0:T(8,128)(2,1)} %copy.134) | copy-start | bytes 786436 | tf_op jit(solution)/shard_map/while
  233.6 4.0 copy-start.1
  293.8 7.4 %copy-start.3 = (bf16[2,48,64,256]{3,2,1,0:T(8,128)(2,1)S(1)}, bf16[2,48,64,256]{3,2,1,0:T(8,128)(2,1)}, u32[]{:S(2)}) copy-start(bf16[2,48,64,256]{3,2,1,0:T(8,128)(2,1)} %copy-done.2) | copy-start | bytes 9437188 | tf_op jit(solution)/shard_map/while
  315.2 48.5 %collective-permute-start.3 = (f32[16,2,64,256]{3,2,1,0:T(8,128)}, f32[16,2,64,256]{3,2,1,0:T(8,128)}, u32[]{:S(2)}, u32[]{:S(2)}) collective-permute-start(f32[16,2,64,256]{3,2,1,0:T(8,128)} %bitcast.59), channel_id=1, source_target_pairs={{0,8},{8,16},{16,24},{24,0},{1,9},{9,17},{17,25},{25,1},{2,10},{10... | collective-permute-start | bytes 6291464 | tf_op jit(solution)/shard_map/ppermute | solution.py:17
  316.5 92.3 %collective-permute-start.2 = (f32[16,2,64,256]{3,2,1,0:T(8,128)}, f32[16,2,64,256]{3,2,1,0:T(8,128)}, u32[]{:S(2)}, u32[]{:S(2)}) collective-permute-start(f32[16,2,64,256]{3,2,1,0:T(8,128)} %bitcast.56), channel_id=1, source_target_pairs={{0,24},{8,0},{16,8},{24,16},{1,25},{9,1},{17,9},{25,17},{2,26},{10... | collective-permute-start | bytes 6291464 | tf_op jit(solution)/shard_map/ppermute | solution.py:17
  321.3 91.1 %all-to-all-start.4 = ((bf16[4,256,256]{1,2,0:T(8,128)(2,1)}), bf16[4,256,256]{1,2,0:T(8,128)(2,1)S(1)}, u32[]{:S(2)}, u32[]{:S(2)}) async-start(bf16[4,256,256]{1,2,0:T(8,128)(2,1)} %copy.111), calls=%async_computation.4 | async-start | bytes 1048576 | tf_op jit(solution)/shard_map/all_to_all | solution.py:118
  423.7 12.5 %all-to-all-start.6 = ((bf16[4,256,256]{2,1,0:T(8,128)(2,1)}), bf16[4,256,256]{2,1,0:T(8,128)(2,1)S(1)}, u32[]{:S(2)}, u32[]{:S(2)}) async-start(bf16[4,256,256]{2,1,0:T(8,128)(2,1)} %bitcast.28), calls=%async_computation.6 | async-start | bytes 1048576 | tf_op jit(solution)/shard_map/all_to_all | solution.py:120
  (7 other events, 15.2 us)
where the time goes:
time: 441 us; the launch traced here: 437 us
  local copies, waits for them, and re-layouts  190 us (43%)
  waiting for transfers between devices  134 us (30%)
  matrix products  36.1 us (8%)
  starting transfers between devices  33.9 us (8%)
  other arithmetic  29.9 us (7%)
  blocking collectives  11.2 us (3%)
    ppermute x4, waiting for transfers between devices, from_behind(): return lax.ppermute(value, axis, pairs)  110 us
    reshape x4, local copies, waits for them, and re-layouts, one_group(): jnp.stack((grad_key.reshape(group, NBR, BLOCK_TOK, feat_count), grad_valu...  28.3 us
    another operation x2, local copies, waits for them, and re-layouts, one_group(): jnp.stack((grad_key.reshape(group, NBR, BLOCK_TOK, feat_count), grad_valu...  25.6 us
    gather x4, local copies, waits for them, and re-layouts, one_group(): kv_table[:, chosen].reshape(2, group, NBR * BLOCK_TOK, head_count, HEAD_DIM)  23.8 us
    another operation x2, other arithmetic, one_group(): jnp.stack((grad_key.reshape(group, NBR, BLOCK_TOK, feat_count), grad_valu...  22.6 us
    broadcast_in_dim x2, local copies, waits for them, and re-layouts, body(): lax.map(one_group, jnp.arange(group_count, dtype=jnp.int32))  18.9 us
    dynamic_update_slice x4, local copies, waits for them, and re-layouts, body(): lax.map(one_group, jnp.arange(group_count, dtype=jnp.int32))  15.6 us
    squeeze x2, local copies, waits for them, and re-layouts, one_group(): value_rows = keyval_now[1]  13.1 us
  transfers between devices with their start and end apart: 10, of which 9 were waited for; matrix products, arithmetic and copies ran while one was open for 4% of the time, Pallas kernels for 0%

commit v1 on v0

v1 whole, which is shorter than its diff:
```python
import functools
import math

import jax
import jax.numpy as jnp
from jax import lax
from jax.experimental import pallas as pl
from jax.experimental.pallas import tpu as pltpu
from jax.sharding import PartitionSpec as P

HEAD_DIM = 64
BLOCK_TOK = 64
NBR = 8
REACH = 1
PAIR = 2 * HEAD_DIM
LIST_ROWS = NBR * BLOCK_TOK
SCALE = HEAD_DIM ** -0.5
EXP2_SCALE = SCALE * math.log2(math.e)
VMEM_LIMIT = 48 * 1024 * 1024


def from_behind(value, axis, steps):
    count = lax.axis_size(axis)
    pairs = [(source, (source + steps) % count) for source in range(count)]
    return lax.ppermute(value, axis, pairs)


def call_kernel(kernel, out_shape, in_memory, scratch_shapes=(), **cost):
    outs = jax.tree.map(lambda _: pl.BlockSpec(memory_space=pltpu.VMEM), out_shape)
    return pl.pallas_call(
        kernel,
        out_shape=out_shape,
        in_specs=[pl.BlockSpec(memory_space=space) for space in in_memory],
        out_specs=outs,
        scratch_shapes=list(scratch_shapes),
        compiler_params=pltpu.CompilerParams(vmem_limit_bytes=VMEM_LIMIT),
        cost_estimate=pl.CostEstimate(**cost) if cost else None,
    )


def columns_of(ref, head):
    return ref[:, head * HEAD_DIM : (head + 1) * HEAD_DIM]


def pack_kernel(query_ref, grad_ref, key_ref, value_ref, out_ref):
    rows = query_ref.shape[0]
    for head in range(out_ref.shape[0]):
        out_ref[head, :rows] = jnp.concatenate(
            [columns_of(query_ref, head), columns_of(grad_ref, head)], axis=1
        )
        out_ref[head, rows:] = jnp.concatenate(
            [columns_of(key_ref, head), columns_of(value_ref, head)], axis=1
        )


def unpack_kernel(packed_ref, query_ref, key_ref, value_ref):
    rows = query_ref.shape[0]
    half = rows // 2
    for pair in range(packed_ref.shape[0] // 2):
        lanes = slice(pair * PAIR, (pair + 1) * PAIR)
        even, odd = packed_ref[2 * pair], packed_ref[2 * pair + 1]
        key_ref[:, lanes] = jnp.concatenate([even[:rows, :HEAD_DIM], odd[:rows, :HEAD_DIM]], axis=1)
        value_ref[:, lanes] = jnp.concatenate([even[:rows, HEAD_DIM:], odd[:rows, HEAD_DIM:]], axis=1)
        query_ref[:half, lanes] = jnp.concatenate([even[rows:, :HEAD_DIM], odd[rows:, :HEAD_DIM]], axis=1)
        query_ref[half:, lanes] = jnp.concatenate([even[rows:, HEAD_DIM:], odd[rows:, HEAD_DIM:]], axis=1)


def block_pair_gradients(rows_a, rows_b, list_a, list_b):
    low = lax.broadcasted_iota(jnp.int32, (BLOCK_TOK, PAIR), 1) < HEAD_DIM
    zero = jnp.zeros_like(rows_a)
    diagonal = jnp.concatenate(
        [
            jnp.concatenate([jnp.where(low, rows_a, zero), zero], axis=1),
            jnp.concatenate([zero, jnp.where(low, rows_b, zero)], axis=1),
            jnp.concatenate([jnp.where(low, zero, rows_a), zero], axis=1),
            jnp.concatenate([zero, jnp.where(low, zero, rows_b)], axis=1),
        ],
        axis=0,
    )
    listed = jnp.concatenate([list_a, list_b], axis=1)
    both = lax.dot_general(listed, diagonal, (((1,), (1,)), ((), ())), preferred_element_type=jnp.float32)
    scores, grad_prob = both[:, :PAIR], both[:, PAIR:]
    top = jnp.max(scores, axis=0, keepdims=True)
    weights = jnp.exp2((scores - top) * EXP2_SCALE)
    inverse = 1.0 / jnp.sum(weights, axis=0, keepdims=True)
    row_delta = jnp.sum(weights * grad_prob, axis=0, keepdims=True) * inverse
    probability = weights * inverse
    score_low = (probability * (grad_prob - row_delta)).astype(jnp.bfloat16)
    prob_low = probability.astype(jnp.bfloat16)
    grad_listed = lax.dot_general(
        jnp.concatenate([score_low, prob_low], axis=1),
        diagonal,
        (((1,), (0,)), ((), ())),
        preferred_element_type=jnp.float32,
    )
    grad_query = lax.dot_general(
        score_low, listed, (((0,), (0,)), ((), ())), preferred_element_type=jnp.float32
    )
    return grad_query[:BLOCK_TOK, :PAIR], grad_query[BLOCK_TOK:, PAIR:], grad_listed


def accumulate_blocks(table_ref, nbr_ref, query_rows, key_value_rows, grad_query_ref, acc_ref):
    def gather_list(block):
        picks = [table_ref[nbr_ref[block, n]] for n in range(NBR)]
        return picks, jnp.concatenate([key_value_rows(pick) for pick in picks], axis=0)

    def step(index, carry):
        slot_a, slot_b = table_ref[2 * index], table_ref[2 * index + 1]
        picks_a, list_a = gather_list(2 * index)
        picks_b, list_b = gather_list(2 * index + 1)
        grad_a, grad_b, grad_listed = block_pair_gradients(
            query_rows(slot_a), query_rows(slot_b), list_a, list_b
        )
        grad_query_ref[slot_a] = grad_a * SCALE
        grad_query_ref[slot_b] = grad_b * SCALE
        for n in range(NBR):
            part = slice(n * BLOCK_TOK, (n + 1) * BLOCK_TOK)
            acc_ref[picks_a[n]] += grad_listed[part, :PAIR]
            acc_ref[picks_b[n]] += grad_listed[part, PAIR:]
        return carry

    acc_ref[...] = jnp.zeros_like(acc_ref)
    lax.fori_loop(0, nbr_ref.shape[0] // 2, step, 0)


def key_scale():
    low = lax.broadcasted_iota(jnp.int32, (1, PAIR), 1) < HEAD_DIM
    return jnp.where(low, jnp.float32(SCALE), jnp.float32(1.0))


def head_kernel(table_ref, nbr_ref, packed_ref, out_ref, grad_query_ref, acc_ref):
    sources, double_rows, _ = packed_ref.shape
    rows = double_rows // 2
    half = rows // 2
    per_source = rows // BLOCK_TOK

    def block_rows(first, slot):
        start = pl.multiple_of(first + slot % per_source * BLOCK_TOK, BLOCK_TOK)
        return packed_ref[slot // per_source, pl.ds(start, BLOCK_TOK)]

    accumulate_blocks(
        table_ref,
        nbr_ref,
        functools.partial(block_rows, 0),
        functools.partial(block_rows, rows),
        grad_query_ref,
        acc_ref,
    )

    def write(source, carry):
        for place in range(per_source):
            slot = source * per_source + place
            out_ref[source, place * BLOCK_TOK : (place + 1) * BLOCK_TOK] = (
                acc_ref[slot] * key_scale()
            ).astype(jnp.bfloat16)
        for place in range(per_source // 2):
            slot = source * per_source + place
            both = jnp.concatenate(
                [grad_query_ref[slot][:, :HEAD_DIM], grad_query_ref[slot + per_source // 2][:, :HEAD_DIM]],
                axis=1,
            )
            start = rows + place * BLOCK_TOK
            out_ref[source, start : start + BLOCK_TOK] = both.astype(jnp.bfloat16)
        return carry

    lax.fori_loop(0, sources, write, 0)


def one_head_each(queries, key_states, value_states, grad_output, block_slot, neighbours):
    axes = ("ctx", "head")
    rows, width = queries.shape
    heads = width // HEAD_DIM
    blocks = block_slot.shape[0]
    in_vmem, in_smem = pltpu.VMEM, pltpu.SMEM
    packed = call_kernel(
        pack_kernel,
        jax.ShapeDtypeStruct((heads, 2 * rows, PAIR), jnp.bfloat16),
        [in_vmem] * 4,
    )(queries, grad_output, key_states, value_states)
    packed = lax.all_to_all(packed, axes, split_axis=0, concat_axis=0, tiled=True)
    grads = call_kernel(
        head_kernel,
        jax.ShapeDtypeStruct((heads, 3 * rows // 2, PAIR), jnp.bfloat16),
        [in_smem, in_smem, in_vmem],
        [pltpu.VMEM((blocks, BLOCK_TOK, PAIR), jnp.float32)] * 2,
        flops=10 * blocks * BLOCK_TOK * LIST_ROWS * HEAD_DIM,
        bytes_accessed=7 * heads * rows * PAIR,
        transcendentals=blocks * BLOCK_TOK * LIST_ROWS,
    )(block_slot, neighbours, packed)
    grads = lax.all_to_all(grads, axes, split_axis=0, concat_axis=0, tiled=True)
    return call_kernel(
        unpack_kernel,
        (jax.ShapeDtypeStruct((rows, width), jnp.bfloat16),) * 3,
        [in_vmem],
    )(grads)


def halo_kernel(table_ref, nbr_ref, query_ref, key_value_ref, grad_query_out, acc_out, grad_query_ref, acc_ref):
    for head in range(query_ref.shape[0]):
        accumulate_blocks(
            table_ref,
            nbr_ref,
            lambda slot: query_ref[head, slot],
            lambda slot: key_value_ref[head, slot],
            grad_query_ref,
            acc_ref,
        )
        grad_query_out[head] = grad_query_ref[...]
        acc_out[head] = acc_ref[...] * key_scale()


def halo_exchange(queries, key_states, value_states, grad_output, block_slot, neighbours):
    def to_heads(value):
        return lax.all_to_all(value, "head", split_axis=1, concat_axis=0, tiled=True)

    def paired(left, right):
        parts = [to_heads(x).reshape(-1, BLOCK_TOK, heads, 1, HEAD_DIM) for x in (left, right)]
        both = jnp.concatenate(parts, axis=3)
        return jnp.moveaxis(both, 2, 0).reshape(heads, -1, BLOCK_TOK, PAIR)

    heads = queries.shape[1] // HEAD_DIM // lax.axis_size("head")
    query_side = paired(queries, grad_output)
    key_side = paired(key_states, value_states)
    blocks = query_side.shape[1]
    ctx_size = lax.axis_size("ctx")
    ctx_here = lax.axis_index("ctx")
    slot_ids = jnp.arange(block_slot.shape[0], dtype=jnp.int32)
    matches = (block_slot[None, :] == slot_ids[:, None]).astype(jnp.int32)
    sphere_of = jnp.sum(matches * slot_ids[None, :], axis=1)
    my_slots = ctx_here * blocks + jnp.arange(blocks, dtype=jnp.int32)
    listed = block_slot[neighbours[sphere_of[my_slots]]]
    gap = (listed // blocks - ctx_here + ctx_size + REACH) % ctx_size - REACH
    lookup = (gap + REACH) * blocks + listed % blocks
    offsets = range(-REACH, REACH + 1)
    span = jnp.concatenate(
        [key_side if o == 0 else from_behind(key_side, "ctx", -o) for o in offsets], axis=1
    )
    span_blocks = span.shape[1]
    grad_query, partial = call_kernel(
        halo_kernel,
        (
            jax.ShapeDtypeStruct((heads, blocks, BLOCK_TOK, PAIR), jnp.float32),
            jax.ShapeDtypeStruct((heads, span_blocks, BLOCK_TOK, PAIR), jnp.float32),
        ),
        [pltpu.SMEM, pltpu.SMEM, pltpu.VMEM, pltpu.VMEM],
        [
            pltpu.VMEM((blocks, BLOCK_TOK, PAIR), jnp.float32),
            pltpu.VMEM((span_blocks, BLOCK_TOK, PAIR), jnp.float32),
        ],
    )(jnp.arange(span_blocks, dtype=jnp.int32), lookup.astype(jnp.int32), query_side, span)
    returned = partial.reshape(heads, 2 * REACH + 1, blocks, BLOCK_TOK, PAIR)
    summed = returned[:, REACH]
    for offset in offsets:
        if offset != 0:
            summed = summed + from_behind(returned[:, offset + REACH], "ctx", offset)

    def to_tokens(value):
        value = jnp.moveaxis(value.astype(jnp.bfloat16), 0, 2).reshape(-1, heads * HEAD_DIM)
        return lax.all_to_all(value, "head", split_axis=0, concat_axis=1, tiled=True)

    return (
        to_tokens(grad_query[..., :HEAD_DIM]),
        to_tokens(summed[..., :HEAD_DIM]),
        to_tokens(summed[..., HEAD_DIM:]),
    )


def solution(mesh):
    devices = mesh.shape["ctx"] * mesh.shape["head"]

    def body(queries, *rest):
        rows, width = queries.shape
        one_each = width == devices * HEAD_DIM and rows % (2 * BLOCK_TOK) == 0
        return (one_head_each if one_each else halo_exchange)(queries, *rest)

    tokens = P(("band", "ctx", "head"), None)
    return jax.shard_map(
        body,
        mesh=mesh,
        in_specs=(tokens,) * 4 + (P("band"), P("band", None)),
        out_specs=(tokens,) * 3,
        check_vma=False,
    )
```

time: 441 us -> 132 us (0.30)
  local copies, waits for them, and re-layouts: 190 us -> 4.25 us
  waiting for transfers between devices: 134 us -> 41.4 us
  matrix products: 36.1 us -> 0 us
  blocking collectives: 11.2 us -> 47.1 us
  Pallas kernels: 0 us -> 30.3 us
  other arithmetic: 29.9 us -> 0 us
  starting transfers between devices: 33.9 us -> 7.45 us
    ppermute x4 -> x0, waiting for transfers between devices: 110 us -> none  [from_behind(): return lax.ppermute(value, axis, pairs)]
    all_to_all x1, blocking collectives: 11.2 us -> 47.1 us  [one_head_each(): grads = lax.all_to_all(grads, axes, split_axis=0, concat_axis=0, tiled=True)]
    reshape x6 -> x0, local copies, waits for them, and re-layouts: 31.3 us -> none  [the longest x4 28.3 us: one_group(): jnp.stack((grad_key.reshape(group, NBR, BLOCK_TOK, feat_count), grad_valu...]
    pallas_call x0 -> x3, Pallas kernels: none -> 30.3 us  [the longest x1 26.7 us: one_head_each(): call_kernel(head_kernel, jax.ShapeDtypeStruct((heads, 3 * rows // 2, PAIR...]
    dot_general x9 -> x0, matrix products: 29.7 us -> none  [the longest x1 9.63 us: body(): jnp.dot(selector, contributions, precision=lax.Precision.HIGHEST, preferr...]
    gather x9 -> x0, local copies, waits for them, and re-layouts: 26.4 us -> none  [the longest x4 23.8 us: one_group(): kv_table[:, chosen].reshape(2, group, NBR * BLOCK_TOK, head_count, HEAD_DIM)]
    another operation x2 -> x0, local copies, waits for them, and re-layouts: 25.6 us -> none  [one_group(): jnp.stack((grad_key.reshape(group, NBR, BLOCK_TOK, feat_count), grad_valu...]
    squeeze x4 -> x0, local copies, waits for them, and re-layouts: 23.8 us -> none  [the longest x2 13.1 us: one_group(): value_rows = keyval_now[1]]
  transfers between devices with their start and end apart: 10 -> 1, of which waited for: 9 -> 1; matrix products, arithmetic and copies ran while one was open for 4% -> 0% of each run, Pallas kernels for 0% -> 0%
where the time goes in v1:
time: 132 us; the launch traced here: 131 us
  blocking collectives  47.1 us (36%)
  waiting for transfers between devices  41.4 us (31%)
  Pallas kernels  30.3 us (23%)
  starting transfers between devices  7.45 us (6%)
  local copies, waits for them, and re-layouts  4.25 us (3%)
    all_to_all x1, blocking collectives, one_head_each(): grads = lax.all_to_all(grads, axes, split_axis=0, concat_axis=0, tiled=True)  47.1 us
    all_to_all x1, waiting for transfers between devices, one_head_each(): lax.all_to_all(packed, axes, split_axis=0, concat_axis=0, tiled=True)  41.4 us
    pallas_call x1, Pallas kernels, one_head_each(): call_kernel(head_kernel, jax.ShapeDtypeStruct((heads, 3 * rows // 2, PAIR...  26.7 us
    all_to_all x1, starting transfers between devices, one_head_each(): lax.all_to_all(packed, axes, split_axis=0, concat_axis=0, tiled=True)  7.45 us
    unnamed x13, local copies, waits for them, and re-layouts  4.25 us
  transfers between devices with their start and end apart: 1, of which 1 were waited for; matrix products, arithmetic and copies ran while one was open for 0% of the time, Pallas kernels for 0%

profile of v1, /device:TPU:1, one launch (start us, length us, event | category | flops | bytes accessed | tf_op | source)
XLA Modules:
  0.0 131.1 jit_solution(3441004689198132273)
XLA Ops:
  0.6 0.0 copy-start
  0.6 1.0 copy-done
  1.7 0.0 copy-start.1
  1.7 1.0 copy-done.1
  2.7 0.0 copy-start.2
  2.7 1.0 copy-done.2
  3.8 0.0 copy-start.3
  3.8 1.0 copy-done.3
  4.8 2.0 %shard_map.85 = bf16[16,512,128]{2,1,0:T(8,128)(2,1)} custom-call(bf16[256,1024]{1,0:T(8,128)(2,1)S(1)} %copy-done, bf16[256,1024]{1,0:T(8,128)(2,1)S(1)} %copy-done.1, bf16[256,1024]{1,0:T(8,128)(2,1)S(1)} %copy-done.2, bf16[256,1024]{1,0:T(8,128)(2,1)S(1)} %copy-done.3), custom_call_target="tpu_custom_call" | custom-call | tf_op jit(solution)/shard_map/pallas_call | solution.py:175
  6.8 0.0 copy-start.5
  6.8 0.0 copy-start.4
  6.8 7.5 %all-to-all-start = ((bf16[16,512,128]{2,1,0:T(8,128)(2,1)}), bf16[16,512,128]{2,1,0:T(8,128)(2,1)S(1)}, u32[]{:S(2)}, u32[]{:S(2)}) async-start(bf16[16,512,128]{2,1,0:T(8,128)(2,1)} %shard_map.85), calls=%async_computation | async-start | bytes 4194304 | tf_op jit(solution)/shard_map/all_to_all | solution.py:180
  14.2 0.0 copy-done.5
  14.2 0.1 copy.9.nbr_ref
  14.3 41.4 %all-to-all-done.packed_ref = bf16[16,512,128]{2,1,0:T(8,128)(2,1)S(1)} async-done(((bf16[16,512,128]{2,1,0:T(8,128)(2,1)}), bf16[16,512,128]{2,1,0:T(8,128)(2,1)S(1)}, u32[]{:S(2)}, u32[]{:S(2)}) %all-to-all-start) | async-done | bytes 2097184 | tf_op jit(solution)/shard_map/all_to_all | solution.py:180
  55.7 0.0 copy-done.4
  55.7 26.7 %shard_map.86 = bf16[16,384,128]{2,1,0:T(8,128)(2,1)S(1)} custom-call(s32[64]{0:T(128)S(1)} %copy-done.4, s32[64,8]{1,0:T(8,128)S(1)} %copy.9.nbr_ref, bf16[16,512,128]{2,1,0:T(8,128)(2,1)S(1)} %all-to-all-done.packed_ref), custom_call_target="tpu_custom_call" | custom-call | flops 1342177280 | bytes 3670016 | tf_op jit(solution)/shard_map/pallas_call | solution.py:181
  82.4 47.1 %all_to_all.10.packed_ref = bf16[16,384,128]{2,1,0:T(8,128)(2,1)S(1)} all-to-all(bf16[16,384,128]{2,1,0:T(8,128)(2,1)S(1)} %shard_map.86), channel_id=1, replica_groups=mesh['ctx'=4,'head'=4,'band'=2] {'ctx','head'}, dimensions={0} | all-to-all | bytes 3145728 | tf_op jit(solution)/shard_map/all_to_all | solution.py:190
  129.5 1.6 %shard_map.87 = (bf16[256,1024]{1,0:T(8,128)(2,1)}, bf16[256,1024]{1,0:T(8,128)(2,1)}, bf16[256,1024]{1,0:T(8,128)(2,1)}) custom-call(bf16[16,384,128]{2,1,0:T(8,128)(2,1)S(1)} %all_to_all.10.packed_ref), custom_call_target="tpu_custom_call" | custom-call | tf_op jit(solution)/shard_map/pallas_call | solution.py:191
Async XLA Ops:
  0.6 1.0 copy-start
  1.7 1.0 copy-start.1
  2.7 1.0 copy-start.2
  3.8 1.0 copy-start.3
  6.8 7.5 %copy-start.5 = (s32[64,8]{0,1:T(8,128)S(1)}, s32[64,8]{0,1:T(8,128)}, u32[]{:S(2)}) copy-start(s32[64,8]{0,1:T(8,128)} %param.11) | copy-start | bytes 6148
  6.8 48.9 %copy-start.4 = (s32[64]{0:T(128)S(1)}, s32[64]{0:T(128)}, u32[]{:S(2)}) copy-start(s32[64]{0:T(128)} %table_ref.1) | copy-start | bytes 772
  6.8 48.9 %all-to-all-start = ((bf16[16,512,128]{2,1,0:T(8,128)(2,1)}), bf16[16,512,128]{2,1,0:T(8,128)(2,1)S(1)}, u32[]{:S(2)}, u32[]{:S(2)}) async-start(bf16[16,512,128]{2,1,0:T(8,128)(2,1)} %shard_map.85), calls=%async_computation | async-start | bytes 4194304 | tf_op jit(solution)/shard_map/all_to_all | solution.py:180

commit v2 on v1

v2 whole, which is shorter than its diff:
```python
import math

import jax
import jax.numpy as jnp
from jax import lax
from jax.experimental import pallas as pl
from jax.experimental.pallas import tpu as pltpu
from jax.sharding import PartitionSpec as P

HEAD_DIM = 64
BLOCK_TOK = 64
NBR = 8
REACH = 1
PAIR = 2 * HEAD_DIM
LIST_ROWS = NBR * BLOCK_TOK
SCALE = HEAD_DIM ** -0.5
EXP2_SCALE = SCALE * math.log2(math.e)
SUBLANES = 8
CHUNK = 16
VMEM_LIMIT = 48 * 1024 * 1024
PACK_VMEM_LIMIT = 60 * 1024 * 1024
NT = (((1,), (1,)), ((), ()))
NN = (((1,), (0,)), ((), ()))
TN = (((0,), (0,)), ((), ()))


def from_behind(value, axis, steps):
    count = lax.axis_size(axis)
    pairs = [(source, (source + steps) % count) for source in range(count)]
    return lax.ppermute(value, axis, pairs)


def call_kernel(kernel, out_shape, in_memory, scratch_shapes=(), **cost):
    outs = jax.tree.map(lambda _: pl.BlockSpec(memory_space=pltpu.VMEM), out_shape)
    return pl.pallas_call(
        kernel,
        out_shape=out_shape,
        in_specs=[pl.BlockSpec(memory_space=space) for space in in_memory],
        out_specs=outs,
        scratch_shapes=list(scratch_shapes),
        compiler_params=pltpu.CompilerParams(vmem_limit_bytes=VMEM_LIMIT),
        cost_estimate=pl.CostEstimate(**cost) if cost else None,
    )


def columns_of(ref, head):
    return ref[:, head * HEAD_DIM : (head + 1) * HEAD_DIM]


def pack_kernel(query_ref, grad_ref, key_ref, value_ref, out_ref):
    for head in range(out_ref.shape[0]):
        out_ref[head, 0] = jnp.concatenate([columns_of(query_ref, head), columns_of(grad_ref, head)], axis=1)
        out_ref[head, 1] = jnp.concatenate([columns_of(key_ref, head), columns_of(value_ref, head)], axis=1)


def unpack_kernel(packed_ref, query_ref, key_ref, value_ref):
    rows = query_ref.shape[0]
    for pair in range(packed_ref.shape[0] // 2):
        lanes = slice(pair * PAIR, (pair + 1) * PAIR)
        even, odd = packed_ref[2 * pair], packed_ref[2 * pair + 1]
        key_ref[:, lanes] = jnp.concatenate([even[:rows, :HEAD_DIM], odd[:rows, :HEAD_DIM]], axis=1)
        value_ref[:, lanes] = jnp.concatenate([even[:rows, HEAD_DIM:], odd[:rows, HEAD_DIM:]], axis=1)
        for place in range(rows // (2 * BLOCK_TOK)):
            start = rows + place * BLOCK_TOK
            part = slice(start, start + BLOCK_TOK)
            first = slice(2 * place * BLOCK_TOK, (2 * place + 1) * BLOCK_TOK)
            second = slice((2 * place + 1) * BLOCK_TOK, (2 * place + 2) * BLOCK_TOK)
            query_ref[first, lanes] = jnp.concatenate([even[part, :HEAD_DIM], odd[part, :HEAD_DIM]], axis=1)
            query_ref[second, lanes] = jnp.concatenate([even[part, HEAD_DIM:], odd[part, HEAD_DIM:]], axis=1)


def diagonal_of(rows):
    low = lax.broadcasted_iota(jnp.int32, (BLOCK_TOK, PAIR), 1) < HEAD_DIM
    rows_a, rows_b = rows[:BLOCK_TOK], rows[BLOCK_TOK:]
    zero = jnp.zeros_like(rows_a)
    return jnp.concatenate(
        [
            jnp.concatenate([jnp.where(low, rows_a, zero), zero], axis=1),
            jnp.concatenate([zero, jnp.where(low, rows_b, zero)], axis=1),
            jnp.concatenate([jnp.where(low, zero, rows_a), zero], axis=1),
            jnp.concatenate([zero, jnp.where(low, zero, rows_b)], axis=1),
        ],
        axis=0,
    )


def fold_rows(value, reduce):
    return reduce(value.reshape(-1, SUBLANES, PAIR), axis=0)


def accumulate_blocks(pairs, list_ref, place_ref, query_pair, key_value_rows, write_query, acc_ref, buffers):
    count = 2 * NBR

    def listed_of(pair):
        starts = [pl.multiple_of(list_ref[pair * count + n], BLOCK_TOK) for n in range(count)]
        blocks = [key_value_rows(start) for start in starts]
        return jnp.concatenate(
            [jnp.concatenate(blocks[:NBR], axis=0), jnp.concatenate(blocks[NBR:], axis=0)], axis=1
        )

    def scores_stage(pair, buffer):
        both_ref, _ = buffer
        both_ref[...] = lax.dot_general(
            listed_of(pair), diagonal_of(query_pair(pair)), NT, preferred_element_type=jnp.float32
        )

    def softmax_stage(buffer):
        both_ref, low_ref = buffer
        chunks = [slice(start, start + CHUNK) for start in range(0, LIST_ROWS, CHUNK)]
        top = None
        for rows in chunks:
            part = fold_rows(both_ref[rows, :PAIR], jnp.max)
            top = part if top is None else jnp.maximum(top, part)
        top = jnp.max(top, axis=0, keepdims=True) * EXP2_SCALE
        total = delta = None
        for rows in chunks:
            weights = jnp.exp2(both_ref[rows, :PAIR] * EXP2_SCALE - top)
            part, part_delta = fold_rows(weights, jnp.sum), fold_rows(weights * both_ref[rows, PAIR:], jnp.sum)
            both_ref[rows, :PAIR] = weights
            total = part if total is None else total + part
            delta = part_delta if delta is None else delta + part_delta
        inverse = 1.0 / jnp.sum(total, axis=0, keepdims=True)
        row_delta = jnp.sum(delta, axis=0, keepdims=True) * inverse
        for rows in chunks:
            probability = both_ref[rows, :PAIR] * inverse
            grad_score = probability * (both_ref[rows, PAIR:] - row_delta)
            low_ref[rows, :PAIR] = grad_score.astype(jnp.bfloat16)
            low_ref[rows, PAIR:] = probability.astype(jnp.bfloat16)

    def gradients_stage(pair, buffer):
        _, low_ref = buffer
        grad_listed = lax.dot_general(
            low_ref[...], diagonal_of(query_pair(pair)), NN, preferred_element_type=jnp.float32
        )
        for n in range(NBR):
            for side in range(2):
                start = pl.multiple_of(place_ref[pair * count + side * NBR + n], BLOCK_TOK)
                acc_ref[pl.ds(start, BLOCK_TOK)] += grad_listed[
                    n * BLOCK_TOK : (n + 1) * BLOCK_TOK, side * PAIR : (side + 1) * PAIR
                ]
        grad_query = lax.dot_general(
            low_ref[:, :PAIR], listed_of(pair), TN, preferred_element_type=jnp.float32
        )
        write_query(
            pair,
            jnp.concatenate(
                [grad_query[:BLOCK_TOK, :HEAD_DIM], grad_query[BLOCK_TOK:, PAIR : PAIR + HEAD_DIM]], axis=1
            )
            * SCALE,
        )

    even, odd = buffers[:2], buffers[2:]
    last = pairs - 1
    acc_ref[...] = jnp.zeros_like(acc_ref)
    scores_stage(0, even)
    softmax_stage(even)
    scores_stage(1, odd)

    def step(index, carry):
        pair = 2 * index
        gradients_stage(pair, even)
        softmax_stage(odd)
        scores_stage(jnp.minimum(pair + 2, last), even)
        gradients_stage(pair + 1, odd)
        softmax_stage(even)
        scores_stage(jnp.minimum(pair + 3, last), odd)
        return carry

    lax.fori_loop(0, pairs // 2, step, 0)


def key_scale():
    low = lax.broadcasted_iota(jnp.int32, (1, PAIR), 1) < HEAD_DIM
    return jnp.where(low, jnp.float32(SCALE), jnp.float32(1.0))


def head_kernel(list_ref, place_ref, packed_ref, out_ref, acc_ref, *buffers):
    sources, out_rows, _ = out_ref.shape
    rows = 2 * out_rows // 3
    pairs_each = rows // (2 * BLOCK_TOK)

    def query_pair(pair):
        start = pair // pairs_each * (2 * rows) + pair % pairs_each * (2 * BLOCK_TOK)
        return packed_ref[pl.ds(pl.multiple_of(start, 2 * BLOCK_TOK), 2 * BLOCK_TOK)]

    def write_query(pair, value):
        start = rows + pl.multiple_of(pair % pairs_each * BLOCK_TOK, BLOCK_TOK)
        out_ref[pair // pairs_each, pl.ds(start, BLOCK_TOK)] = value.astype(jnp.bfloat16)

    accumulate_blocks(
        sources * pairs_each,
        list_ref,
        place_ref,
        query_pair,
        lambda start: packed_ref[pl.ds(start, BLOCK_TOK)],
        write_query,
        acc_ref,
        buffers,
    )

    def write(source, carry):
        start = pl.multiple_of(source * rows, rows)
        out_ref[source, :rows] = (acc_ref[pl.ds(start, rows)] * key_scale()).astype(jnp.bfloat16)
        return carry

    lax.fori_loop(0, sources, write, 0)


def work_buffers():
    return [
        pltpu.VMEM((LIST_ROWS, 2 * PAIR), jnp.float32),
        pltpu.VMEM((LIST_ROWS, 2 * PAIR), jnp.bfloat16),
    ] * 2


def listed_slots(block_slot, neighbours):
    slot_ids = jnp.arange(block_slot.shape[0], dtype=jnp.int32)
    matches = (block_slot[None, :] == slot_ids[:, None]).astype(jnp.int32)
    sphere_of = jnp.sum(matches * slot_ids[None, :], axis=1)
    return block_slot[neighbours[sphere_of]]


def one_head_each(queries, key_states, value_states, grad_output, block_slot, neighbours):
    axes = ("ctx", "head")
    rows, width = queries.shape
    heads = width // HEAD_DIM
    tokens = heads * rows
    in_vmem, in_smem = pltpu.VMEM, pltpu.SMEM
    packed = pl.pallas_call(
        pack_kernel,
        grid=(2,),
        in_specs=[pl.BlockSpec((rows // 2, width), lambda i: (i, 0))] * 4,
        out_specs=pl.BlockSpec((heads, 2, rows // 2, PAIR), lambda i: (0, 0, i, 0)),
        out_shape=jax.ShapeDtypeStruct((heads, 2, rows, PAIR), jnp.bfloat16),
        compiler_params=pltpu.CompilerParams(vmem_limit_bytes=PACK_VMEM_LIMIT),
    )(queries, grad_output, key_states, value_states)
    packed = lax.all_to_all(packed, axes, split_axis=0, concat_axis=0, tiled=True)
    place = listed_slots(block_slot, neighbours).reshape(-1) * BLOCK_TOK
    start = place // rows * (2 * rows) + rows + place % rows
    grads = call_kernel(
        head_kernel,
        jax.ShapeDtypeStruct((heads, 3 * rows // 2, PAIR), jnp.bfloat16),
        [in_smem, in_smem, in_vmem],
        [pltpu.VMEM((tokens, PAIR), jnp.float32)] + work_buffers(),
        flops=10 * tokens * LIST_ROWS * HEAD_DIM,
        bytes_accessed=7 * tokens * PAIR,
        transcendentals=tokens * LIST_ROWS,
    )(start, place, packed.reshape(2 * tokens, PAIR))
    grads = lax.all_to_all(grads, axes, split_axis=0, concat_axis=0, tiled=True)
    return call_kernel(
        unpack_kernel,
        (jax.ShapeDtypeStruct((rows, width), jnp.bfloat16),) * 3,
        [in_vmem],
    )(grads)


def halo_kernel(list_ref, query_ref, key_value_ref, grad_query_out, acc_out, *buffers):
    for head in range(query_ref.shape[0]):

        def write_query(pair, value):
            grad_query_out[head, pl.ds(pl.multiple_of(pair * BLOCK_TOK, BLOCK_TOK), BLOCK_TOK)] = value

        accumulate_blocks(
            query_ref.shape[1] // (2 * BLOCK_TOK),
            list_ref,
            list_ref,
            lambda pair: query_ref[head, pl.ds(pl.multiple_of(pair * 2 * BLOCK_TOK, 2 * BLOCK_TOK), 2 * BLOCK_TOK)],
            lambda start: key_value_ref[head, pl.ds(start, BLOCK_TOK)],
            write_query,
            acc_out.at[head],
            buffers,
        )
        acc_out[head] = acc_out[head] * key_scale()


def halo_exchange(queries, key_states, value_states, grad_output, block_slot, neighbours):
    def to_heads(value):
        return lax.all_to_all(value, "head", split_axis=1, concat_axis=0, tiled=True)

    def paired(left, right):
        parts = [to_heads(x).reshape(-1, heads, 1, HEAD_DIM) for x in (left, right)]
        both = jnp.concatenate(parts, axis=2)
        return jnp.moveaxis(both, 1, 0).reshape(heads, -1, PAIR)

    heads = queries.shape[1] // HEAD_DIM // lax.axis_size("head")
    query_side = paired(queries, grad_output)
    key_side = paired(key_states, value_states)
    rows = query_side.shape[1]
    blocks = rows // BLOCK_TOK
    ctx_size = lax.axis_size("ctx")
    ctx_here = lax.axis_index("ctx")
    listed = lax.dynamic_slice_in_dim(listed_slots(block_slot, neighbours), ctx_here * blocks, blocks, 0)
    gap = (listed // blocks - ctx_here + ctx_size + REACH) % ctx_size - REACH
    lookup = (gap + REACH) * blocks + listed % blocks
    offsets = range(-REACH, REACH + 1)
    span = jnp.concatenate(
        [key_side if o == 0 else from_behind(key_side, "ctx", -o) for o in offsets], axis=1
    )
    grad_query, partial = call_kernel(
        halo_kernel,
        (
            jax.ShapeDtypeStruct((heads, rows // 2, PAIR), jnp.float32),
            jax.ShapeDtypeStruct(span.shape, jnp.float32),
        ),
        [pltpu.SMEM, pltpu.VMEM, pltpu.VMEM],
        work_buffers(),
    )(lookup.reshape(-1) * BLOCK_TOK, query_side, span)
    returned = partial.reshape(heads, 2 * REACH + 1, rows, PAIR)
    summed = returned[:, REACH]
    for offset in offsets:
        if offset != 0:
            summed = summed + from_behind(returned[:, offset + REACH], "ctx", offset)

    def to_tokens(value):
        value = jnp.moveaxis(value.astype(jnp.bfloat16), 0, 1).reshape(rows, heads * HEAD_DIM)
        return lax.all_to_all(value, "head", split_axis=0, concat_axis=1, tiled=True)

    grad_query = grad_query.reshape(heads, blocks // 2, BLOCK_TOK, 2, HEAD_DIM)
    return (
        to_tokens(jnp.swapaxes(grad_query, 2, 3).reshape(heads, rows, HEAD_DIM)),
        to_tokens(summed[..., :HEAD_DIM]),
        to_tokens(summed[..., HEAD_DIM:]),
    )


def solution(mesh):
    devices = mesh.shape["ctx"] * mesh.shape["head"]

    def body(queries, *rest):
        rows, width = queries.shape
        one_each = width == devices * HEAD_DIM and rows % (4 * BLOCK_TOK) == 0
        return (one_head_each if one_each else halo_exchange)(queries, *rest)

    tokens = P(("band", "ctx", "head"), None)
    return jax.shard_map(
        body,
        mesh=mesh,
        in_specs=(tokens,) * 4 + (P("band"), P("band", None)),
        out_specs=(tokens,) * 3,
        check_vma=False,
    )
```

time: 132 us -> 113 us (0.86)
  Pallas kernels: 30.3 us -> 16.5 us
  waiting for transfers between devices: 41.4 us -> 37.2 us
    pallas_call x1, Pallas kernels: 26.7 us -> 12 us  [one_head_each(): call_kernel(head_kernel, jax.ShapeDtypeStruct((heads, 3 * rows // 2, PAIR...]
    all_to_all x1, waiting for transfers between devices: 41.4 us -> 37.2 us  [one_head_each(): lax.all_to_all(packed, axes, split_axis=0, concat_axis=0, tiled=True)]
    unnamed x13 -> x5, local copies, waits for them, and re-layouts: 4.25 us -> 0.09 us
    gather x0 -> x2, local copies, waits for them, and re-layouts: none -> 3.95 us  [listed_slots(): return block_slot[neighbours[sphere_of]]]
  transfers between devices with their start and end apart: 1 -> 1, of which waited for: 1 -> 1; matrix products, arithmetic and copies ran while one was open for 0% -> 4% of each run, Pallas kernels for 0% -> 0%
where the time goes in v2:
time: 113 us
  blocking collectives  47.1 us (42%)
  waiting for transfers between devices  37.2 us (33%)
  Pallas kernels  16.5 us (15%)
  starting transfers between devices  7.46 us (7%)
  local copies, waits for them, and re-layouts  4.13 us (4%)
    all_to_all x1, blocking collectives, one_head_each(): grads = lax.all_to_all(grads, axes, split_axis=0, concat_axis=0, tiled=True)  47.1 us
    all_to_all x1, waiting for transfers between devices, one_head_each(): lax.all_to_all(packed, axes, split_axis=0, concat_axis=0, tiled=True)  37.2 us
    pallas_call x1, Pallas kernels, one_head_each(): call_kernel(head_kernel, jax.ShapeDtypeStruct((heads, 3 * rows // 2, PAIR...  12 us
    all_to_all x1, starting transfers between devices, one_head_each(): lax.all_to_all(packed, axes, split_axis=0, concat_axis=0, tiled=True)  7.46 us
    gather x2, local copies, waits for them, and re-layouts, listed_slots(): return block_slot[neighbours[sphere_of]]  3.95 us
    pallas_call x1, Pallas kernels, one_head_each(): pl.pallas_call(pack_kernel, grid=(2,), in_specs=[pl.BlockSpec((rows // 2,...  2.94 us
  transfers between devices with their start and end apart: 1, of which 1 were waited for; matrix products, arithmetic and copies ran while one was open for 4% of the time, Pallas kernels for 0%

profile of v2, /device:TPU:1, one launch (start us, length us, event | category | flops | bytes accessed | tf_op | source)
XLA Modules:
  0.0 113.2 jit_solution(1708851662192257894)
XLA Ops:
  0.6 2.9 %shard_map.85 = bf16[16,2,256,128]{3,2,1,0:T(8,128)(2,1)} custom-call(bf16[256,1024]{1,0:T(8,128)(2,1)} %query_ref.1, bf16[256,1024]{1,0:T(8,128)(2,1)} %grad_ref.1, bf16[256,1024]{1,0:T(8,128)(2,1)} %key_ref.1, bf16[256,1024]{1,0:T(8,128)(2,1)} %value_ref.1), custom_call_target="tpu_custom_call" | custom-call | tf_op jit(solution)/shard_map/pallas_call | solution.py:229
  3.6 0.0 copy-start.1
  3.6 0.0 copy-start
  3.6 7.5 %all-to-all-start = ((bf16[16,2,256,128]{3,2,1,0:T(8,128)(2,1)}), bf16[16,2,256,128]{3,2,1,0:T(8,128)(2,1)S(1)}, u32[]{:S(2)}, u32[]{:S(2)}) async-start(bf16[16,2,256,128]{3,2,1,0:T(8,128)(2,1)} %shard_map.85), calls=%async_computation | async-start | bytes 4194304 | tf_op jit(solution)/shard_map/all_to_all | solution.py:237
  11.0 0.0 copy-done.1
  11.0 0.1 copy.11
  11.1 0.0 copy-done
  11.1 0.1 select_reduce_fusion
  11.3 0.6 gather_fusion
  11.9 0.1 reshape.50
  12.0 3.3 %gather_fusion.1 = s32[512]{0:T(512)S(1)} fusion(s32[64]{0:T(128)S(1)} %copy-done, s32[1024]{0:T(1024)S(1)} %pad_clamp_fusion), kind=kCustom, calls=%fused_computation.1 | custom fusion | bytes 6144 | tf_op jit(solution)/shard_map/gather | solution.py:220
  15.3 37.2 %all-to-all-done = bf16[16,2,256,128]{3,2,1,0:T(8,128)(2,1)S(1)} async-done(((bf16[16,2,256,128]{3,2,1,0:T(8,128)(2,1)}), bf16[16,2,256,128]{3,2,1,0:T(8,128)(2,1)S(1)}, u32[]{:S(2)}, u32[]{:S(2)}) %all-to-all-start) | async-done | bytes 2097184 | tf_op jit(solution)/shard_map/all_to_all | solution.py:237
  52.5 12.0 %shard_map.86 = bf16[16,384,128]{2,1,0:T(8,128)(2,1)S(1)} custom-call(s32[512]{0:T(512)S(1)} %get-tuple-element.4.list_ref, s32[512]{0:T(512)S(1)} %get-tuple-element.3.place_ref, bf16[8192,128]{1,0:T(8,128)(2,1)S(1)} %bitcast.9), custom_call_target="tpu_custom_call" | custom-call | flops 1342177280 | bytes 3670016 | tf_op jit(solution)/shard_map/pallas_call | solution.py:240
  64.5 47.1 %all_to_all.10.packed_ref = bf16[16,384,128]{2,1,0:T(8,128)(2,1)S(1)} all-to-all(bf16[16,384,128]{2,1,0:T(8,128)(2,1)S(1)} %shard_map.86), channel_id=1, replica_groups=mesh['ctx'=4,'head'=4,'band'=2] {'ctx','head'}, dimensions={0} | all-to-all | bytes 3145728 | tf_op jit(solution)/shard_map/all_to_all | solution.py:249
  111.5 1.6 %shard_map.87 = (bf16[256,1024]{1,0:T(8,128)(2,1)}, bf16[256,1024]{1,0:T(8,128)(2,1)}, bf16[256,1024]{1,0:T(8,128)(2,1)}) custom-call(bf16[16,384,128]{2,1,0:T(8,128)(2,1)S(1)} %all_to_all.10.packed_ref), custom_call_target="tpu_custom_call" | custom-call | tf_op jit(solution)/shard_map/pallas_call | solution.py:250
  (5 shorter events, 0.0 us)
Async XLA Ops:
  3.6 7.5 %copy-start.1 = (s32[64,8]{0,1:T(8,128)S(1)}, s32[64,8]{0,1:T(8,128)}, u32[]{:S(2)}) copy-start(s32[64,8]{0,1:T(8,128)} %param.11) | copy-start | bytes 6148
  3.6 7.6 %copy-start = (s32[64]{0:T(128)S(1)}, s32[64]{0:T(128)}, u32[]{:S(2)}) copy-start(s32[64]{0:T(128)} %param.10) | copy-start | bytes 772
  3.6 48.9 %all-to-all-start = ((bf16[16,2,256,128]{3,2,1,0:T(8,128)(2,1)}), bf16[16,2,256,128]{3,2,1,0:T(8,128)(2,1)S(1)}, u32[]{:S(2)}, u32[]{:S(2)}) async-start(bf16[16,2,256,128]{3,2,1,0:T(8,128)(2,1)} %shard_map.85), calls=%async_computation | async-start | bytes 4194304 | tf_op jit(solution)/shard_map/all_to_all | solution.py:237

commit v3 on v2

--- a/solution.py
+++ b/solution.py
@@ -84,11 +84,17 @@
     )
 
 
+def swap_halves(rows):
+    return jnp.concatenate([rows[:, HEAD_DIM:], rows[:, :HEAD_DIM]], axis=1)
+
+
 def fold_rows(value, reduce):
     return reduce(value.reshape(-1, SUBLANES, PAIR), axis=0)
 
 
-def accumulate_blocks(pairs, list_ref, place_ref, query_pair, key_value_rows, write_query, acc_ref, buffers):
+def accumulate_blocks(
+    pairs, list_ref, place_ref, query_pair, key_value_rows, value_key_rows, write_query, acc_ref, buffers
+):
     count = 2 * NBR
 
     def listed_of(pair):
@@ -96,6 +102,17 @@
         blocks = [key_value_rows(start) for start in starts]
         return jnp.concatenate(
             [jnp.concatenate(blocks[:NBR], axis=0), jnp.concatenate(blocks[NBR:], axis=0)], axis=1
+        )
+
+    def listed_keys(pair):
+        low = lax.broadcasted_iota(jnp.int32, (BLOCK_TOK, PAIR), 1) < HEAD_DIM
+        starts = [pl.multiple_of(list_ref[pair * count + n], BLOCK_TOK) for n in range(count)]
+        return jnp.concatenate(
+            [
+                jnp.where(low, key_value_rows(starts[n]), value_key_rows(starts[NBR + n]))
+                for n in range(NBR)
+            ],
+            axis=0,
         )
 
     def scores_stage(pair, buffer):
@@ -139,18 +156,12 @@
                     n * BLOCK_TOK : (n + 1) * BLOCK_TOK, side * PAIR : (side + 1) * PAIR
                 ]
         grad_query = lax.dot_general(
-            low_ref[:, :PAIR], listed_of(pair), TN, preferred_element_type=jnp.float32
-        )
-        write_query(
-            pair,
-            jnp.concatenate(
-                [grad_query[:BLOCK_TOK, :HEAD_DIM], grad_query[BLOCK_TOK:, PAIR : PAIR + HEAD_DIM]], axis=1
-            )
-            * SCALE,
-        )
+            low_ref[:, :PAIR], listed_keys(pair), TN, preferred_element_type=jnp.float32
+        )
+        low = lax.broadcasted_iota(jnp.int32, (BLOCK_TOK, PAIR), 1) < HEAD_DIM
+        write_query(pair, jnp.where(low, grad_query[:BLOCK_TOK], grad_query[BLOCK_TOK:]) * SCALE)
 
     even, odd = buffers[:2], buffers[2:]
-    last = pairs - 1
     acc_ref[...] = jnp.zeros_like(acc_ref)
     scores_stage(0, even)
     softmax_stage(even)
@@ -160,13 +171,16 @@
         pair = 2 * index
         gradients_stage(pair, even)
         softmax_stage(odd)
-        scores_stage(jnp.minimum(pair + 2, last), even)
+        scores_stage(pair + 2, even)
         gradients_stage(pair + 1, odd)
         softmax_stage(even)
-        scores_stage(jnp.minimum(pair + 3, last), odd)
+        scores_stage(pair + 3, odd)
         return carry
 
-    lax.fori_loop(0, pairs // 2, step, 0)
+    lax.fori_loop(0, pairs // 2 - 1, step, 0)
+    gradients_stage(pairs - 2, even)
+    softmax_stage(odd)
+    gradients_stage(pairs - 1, odd)
 
 
 def key_scale():
@@ -174,7 +188,7 @@
     return jnp.where(low, jnp.float32(SCALE), jnp.float32(1.0))
 
 
-def head_kernel(list_ref, place_ref, packed_ref, out_ref, acc_ref, *buffers):
+def head_kernel(list_ref, place_ref, packed_ref, out_ref, acc_ref, swap_ref, *buffers):
     sources, out_rows, _ = out_ref.shape
     rows = 2 * out_rows // 3
     pairs_each = rows // (2 * BLOCK_TOK)
@@ -187,12 +201,16 @@
         start = rows + pl.multiple_of(pair % pairs_each * BLOCK_TOK, BLOCK_TOK)
         out_ref[pair // pairs_each, pl.ds(start, BLOCK_TOK)] = value.astype(jnp.bfloat16)
 
+    for source in range(sources):
+        part = slice((2 * source + 1) * rows, (2 * source + 2) * rows)
+        swap_ref[part] = swap_halves(packed_ref[part])
     accumulate_blocks(
         sources * pairs_each,
         list_ref,
         place_ref,
         query_pair,
         lambda start: packed_ref[pl.ds(start, BLOCK_TOK)],
+        lambda start: swap_ref[pl.ds(start, BLOCK_TOK)],
         write_query,
         acc_ref,
         buffers,
@@ -241,7 +259,8 @@
         head_kernel,
         jax.ShapeDtypeStruct((heads, 3 * rows // 2, PAIR), jnp.bfloat16),
         [in_smem, in_smem, in_vmem],
-        [pltpu.VMEM((tokens, PAIR), jnp.float32)] + work_buffers(),
+        [pltpu.VMEM((tokens, PAIR), jnp.float32), pltpu.VMEM((2 * tokens, PAIR), jnp.bfloat16)]
+        + work_buffers(),
         flops=10 * tokens * LIST_ROWS * HEAD_DIM,
         bytes_accessed=7 * tokens * PAIR,
         transcendentals=tokens * LIST_ROWS,
@@ -254,8 +273,9 @@
     )(grads)
 
 
-def halo_kernel(list_ref, query_ref, key_value_ref, grad_query_out, acc_out, *buffers):
+def halo_kernel(list_ref, query_ref, key_value_ref, grad_query_out, acc_out, swap_ref, *buffers):
     for head in range(query_ref.shape[0]):
+        swap_ref[...] = swap_halves(key_value_ref[head])
 
         def write_query(pair, value):
             grad_query_out[head, pl.ds(pl.multiple_of(pair * BLOCK_TOK, BLOCK_TOK), BLOCK_TOK)] = value
@@ -266,6 +286,7 @@
             list_ref,
             lambda pair: query_ref[head, pl.ds(pl.multiple_of(pair * 2 * BLOCK_TOK, 2 * BLOCK_TOK), 2 * BLOCK_TOK)],
             lambda start: key_value_ref[head, pl.ds(start, BLOCK_TOK)],
+            lambda start: swap_ref[pl.ds(start, BLOCK_TOK)],
             write_query,
             acc_out.at[head],
             buffers,
@@ -303,7 +324,7 @@
             jax.ShapeDtypeStruct(span.shape, jnp.float32),
         ),
         [pltpu.SMEM, pltpu.VMEM, pltpu.VMEM],
-        work_buffers(),
+        [pltpu.VMEM(span.shape[1:], jnp.bfloat16)] + work_buffers(),
     )(lookup.reshape(-1) * BLOCK_TOK, query_side, span)
     returned = partial.reshape(heads, 2 * REACH + 1, rows, PAIR)
     summed = returned[:, REACH]

time: 113 us -> 112 us (level)
  Pallas kernels: 16.5 us -> 15.3 us
    pallas_call x1, Pallas kernels: 12 us -> 10.7 us  [one_head_each(): call_kernel(head_kernel, jax.ShapeDtypeStruct((heads, 3 * rows // 2, PAIR...]
where the time goes in v3:
time: 112 us
  blocking collectives  47.1 us (42%)
  waiting for transfers between devices  37.2 us (33%)
  Pallas kernels  15.3 us (14%)
  starting transfers between devices  7.46 us (7%)
  local copies, waits for them, and re-layouts  4.13 us (4%)
    all_to_all x1, blocking collectives, one_head_each(): grads = lax.all_to_all(grads, axes, split_axis=0, concat_axis=0, tiled=True)  47.1 us
    all_to_all x1, waiting for transfers between devices, one_head_each(): lax.all_to_all(packed, axes, split_axis=0, concat_axis=0, tiled=True)  37.2 us
    pallas_call x1, Pallas kernels, one_head_each(): call_kernel(head_kernel, jax.ShapeDtypeStruct((heads, 3 * rows // 2, PAIR...  10.7 us
    all_to_all x1, starting transfers between devices, one_head_each(): lax.all_to_all(packed, axes, split_axis=0, concat_axis=0, tiled=True)  7.46 us
    gather x2, local copies, waits for them, and re-layouts, listed_slots(): return block_slot[neighbours[sphere_of]]  3.95 us
    pallas_call x1, Pallas kernels, one_head_each(): pl.pallas_call(pack_kernel, grid=(2,), in_specs=[pl.BlockSpec((rows // 2,...  2.94 us
  transfers between devices with their start and end apart: 1, of which 1 were waited for; matrix products, arithmetic and copies ran while one was open for 4% of the time, Pallas kernels for 0%

profile of v3, /device:TPU:1, one launch (start us, length us, event | category | flops | bytes accessed | tf_op | source)
XLA Modules:
  0.0 112.0 jit_solution(4490897932549900524)
XLA Ops:
  0.6 2.9 %shard_map.85 = bf16[16,2,256,128]{3,2,1,0:T(8,128)(2,1)} custom-call(bf16[256,1024]{1,0:T(8,128)(2,1)} %query_ref.1, bf16[256,1024]{1,0:T(8,128)(2,1)} %grad_ref.1, bf16[256,1024]{1,0:T(8,128)(2,1)} %key_ref.1, bf16[256,1024]{1,0:T(8,128)(2,1)} %value_ref.1), custom_call_target="tpu_custom_call" | custom-call | tf_op jit(solution)/shard_map/pallas_call | solution.py:247
  3.6 0.0 copy-start.1
  3.6 0.0 copy-start
  3.6 7.5 %all-to-all-start = ((bf16[16,2,256,128]{3,2,1,0:T(8,128)(2,1)}), bf16[16,2,256,128]{3,2,1,0:T(8,128)(2,1)S(1)}, u32[]{:S(2)}, u32[]{:S(2)}) async-start(bf16[16,2,256,128]{3,2,1,0:T(8,128)(2,1)} %shard_map.85), calls=%async_computation | async-start | bytes 4194304 | tf_op jit(solution)/shard_map/all_to_all | solution.py:255
  11.0 0.0 copy-done.1
  11.0 0.1 copy.11
  11.1 0.0 copy-done
  11.1 0.1 select_reduce_fusion
  11.3 0.6 gather_fusion
  11.9 0.1 reshape.50
  12.0 3.3 %gather_fusion.1 = s32[512]{0:T(512)S(1)} fusion(s32[64]{0:T(128)S(1)} %copy-done, s32[1024]{0:T(1024)S(1)} %pad_clamp_fusion), kind=kCustom, calls=%fused_computation.1 | custom fusion | bytes 6144 | tf_op jit(solution)/shard_map/gather | solution.py:238
  15.3 37.2 %all-to-all-done = bf16[16,2,256,128]{3,2,1,0:T(8,128)(2,1)S(1)} async-done(((bf16[16,2,256,128]{3,2,1,0:T(8,128)(2,1)}), bf16[16,2,256,128]{3,2,1,0:T(8,128)(2,1)S(1)}, u32[]{:S(2)}, u32[]{:S(2)}) %all-to-all-start) | async-done | bytes 2097184 | tf_op jit(solution)/shard_map/all_to_all | solution.py:255
  52.5 10.7 %shard_map.86 = bf16[16,384,128]{2,1,0:T(8,128)(2,1)S(1)} custom-call(s32[512]{0:T(512)S(1)} %get-tuple-element.4.list_ref, s32[512]{0:T(512)S(1)} %get-tuple-element.3.place_ref, bf16[8192,128]{1,0:T(8,128)(2,1)S(1)} %bitcast.9), custom_call_target="tpu_custom_call" | custom-call | flops 1342177280 | bytes 3670016 | tf_op jit(solution)/shard_map/pallas_call | solution.py:258
  63.2 47.1 %all_to_all.10.packed_ref = bf16[16,384,128]{2,1,0:T(8,128)(2,1)S(1)} all-to-all(bf16[16,384,128]{2,1,0:T(8,128)(2,1)S(1)} %shard_map.86), channel_id=1, replica_groups=mesh['ctx'=4,'head'=4,'band'=2] {'ctx','head'}, dimensions={0} | all-to-all | bytes 3145728 | tf_op jit(solution)/shard_map/all_to_all | solution.py:268
  110.3 1.6 %shard_map.87 = (bf16[256,1024]{1,0:T(8,128)(2,1)}, bf16[256,1024]{1,0:T(8,128)(2,1)}, bf16[256,1024]{1,0:T(8,128)(2,1)}) custom-call(bf16[16,384,128]{2,1,0:T(8,128)(2,1)S(1)} %all_to_all.10.packed_ref), custom_call_target="tpu_custom_call" | custom-call | tf_op jit(solution)/shard_map/pallas_call | solution.py:269
  (5 shorter events, 0.0 us)
Async XLA Ops:
  3.6 7.5 %copy-start.1 = (s32[64,8]{0,1:T(8,128)S(1)}, s32[64,8]{0,1:T(8,128)}, u32[]{:S(2)}) copy-start(s32[64,8]{0,1:T(8,128)} %param.11) | copy-start | bytes 6148
  3.6 7.6 %copy-start = (s32[64]{0:T(128)S(1)}, s32[64]{0:T(128)}, u32[]{:S(2)}) copy-start(s32[64]{0:T(128)} %param.10) | copy-start | bytes 772
  3.6 48.9 %all-to-all-start = ((bf16[16,2,256,128]{3,2,1,0:T(8,128)(2,1)}), bf16[16,2,256,128]{3,2,1,0:T(8,128)(2,1)S(1)}, u32[]{:S(2)}, u32[]{:S(2)}) async-start(bf16[16,2,256,128]{3,2,1,0:T(8,128)(2,1)} %shard_map.85), calls=%async_computation | async-start | bytes 4194304 | tf_op jit(solution)/shard_map/all_to_all | solution.py:255

commit v4 on v3

--- a/solution.py
+++ b/solution.py
@@ -16,7 +16,7 @@
 SCALE = HEAD_DIM ** -0.5
 EXP2_SCALE = SCALE * math.log2(math.e)
 SUBLANES = 8
-CHUNK = 16
+CHUNK = 32
 VMEM_LIMIT = 48 * 1024 * 1024
 PACK_VMEM_LIMIT = 60 * 1024 * 1024
 NT = (((1,), (1,)), ((), ()))
@@ -53,20 +53,34 @@
         out_ref[head, 1] = jnp.concatenate([columns_of(key_ref, head), columns_of(value_ref, head)], axis=1)
 
 
-def unpack_kernel(packed_ref, query_ref, key_ref, value_ref):
-    rows = query_ref.shape[0]
-    for pair in range(packed_ref.shape[0] // 2):
-        lanes = slice(pair * PAIR, (pair + 1) * PAIR)
-        even, odd = packed_ref[2 * pair], packed_ref[2 * pair + 1]
-        key_ref[:, lanes] = jnp.concatenate([even[:rows, :HEAD_DIM], odd[:rows, :HEAD_DIM]], axis=1)
-        value_ref[:, lanes] = jnp.concatenate([even[:rows, HEAD_DIM:], odd[:rows, HEAD_DIM:]], axis=1)
-        for place in range(rows // (2 * BLOCK_TOK)):
-            start = rows + place * BLOCK_TOK
-            part = slice(start, start + BLOCK_TOK)
-            first = slice(2 * place * BLOCK_TOK, (2 * place + 1) * BLOCK_TOK)
-            second = slice((2 * place + 1) * BLOCK_TOK, (2 * place + 2) * BLOCK_TOK)
-            query_ref[first, lanes] = jnp.concatenate([even[part, :HEAD_DIM], odd[part, :HEAD_DIM]], axis=1)
-            query_ref[second, lanes] = jnp.concatenate([even[part, HEAD_DIM:], odd[part, HEAD_DIM:]], axis=1)
+def unpack_kernel(packed_ref, query_ref, key_ref, value_ref, held, sems):
+    rows, width = query_ref.shape
+    heads = packed_ref.shape[0]
+
+    def halves(pair, part, lanes):
+        return jnp.concatenate([packed_ref[2 * pair, part, lanes], packed_ref[2 * pair + 1, part, lanes]], axis=1)
+
+    def columns(pair):
+        return slice(pair * PAIR, (pair + 1) * PAIR)
+
+    copies = []
+    first, second = slice(0, HEAD_DIM), slice(HEAD_DIM, PAIR)
+    for n, (out_ref, lanes) in enumerate(((key_ref, first), (value_ref, second))):
+        for pair in range(heads // 2):
+            held[n, :, columns(pair)] = halves(pair, slice(0, rows), lanes)
+        copies.append(pltpu.make_async_copy(held.at[n], out_ref, sems.at[n]))
+        copies[-1].start()
+    for place in range(rows // BLOCK_TOK):
+        start = rows + place // 2 * BLOCK_TOK
+        lanes = second if place % 2 else first
+        for pair in range(heads // 2):
+            held[2, place * BLOCK_TOK : (place + 1) * BLOCK_TOK, columns(pair)] = halves(
+                pair, slice(start, start + BLOCK_TOK), lanes
+            )
+    copies.append(pltpu.make_async_copy(held.at[2], query_ref, sems.at[2]))
+    copies[-1].start()
+    for copy in copies:
+        copy.wait()
 
 
 def diagonal_of(rows):
@@ -116,38 +130,38 @@
         )
 
     def scores_stage(pair, buffer):
-        both_ref, _ = buffer
-        both_ref[...] = lax.dot_general(
+        both_ref, stat_ref = buffer
+        both = lax.dot_general(
             listed_of(pair), diagonal_of(query_pair(pair)), NT, preferred_element_type=jnp.float32
         )
+        both_ref[...] = both
+        stat_ref[...] = fold_rows(both[:, :PAIR], jnp.max)
 
     def softmax_stage(buffer):
-        both_ref, low_ref = buffer
-        chunks = [slice(start, start + CHUNK) for start in range(0, LIST_ROWS, CHUNK)]
-        top = None
-        for rows in chunks:
-            part = fold_rows(both_ref[rows, :PAIR], jnp.max)
-            top = part if top is None else jnp.maximum(top, part)
-        top = jnp.max(top, axis=0, keepdims=True) * EXP2_SCALE
+        both_ref, stat_ref = buffer
+        top = jnp.max(stat_ref[...], axis=0, keepdims=True) * EXP2_SCALE
         total = delta = None
-        for rows in chunks:
+        for start in range(0, LIST_ROWS, CHUNK):
+            rows = slice(start, start + CHUNK)
             weights = jnp.exp2(both_ref[rows, :PAIR] * EXP2_SCALE - top)
             part, part_delta = fold_rows(weights, jnp.sum), fold_rows(weights * both_ref[rows, PAIR:], jnp.sum)
             both_ref[rows, :PAIR] = weights
             total = part if total is None else total + part
             delta = part_delta if delta is None else delta + part_delta
         inverse = 1.0 / jnp.sum(total, axis=0, keepdims=True)
-        row_delta = jnp.sum(delta, axis=0, keepdims=True) * inverse
-        for rows in chunks:
-            probability = both_ref[rows, :PAIR] * inverse
-            grad_score = probability * (both_ref[rows, PAIR:] - row_delta)
-            low_ref[rows, :PAIR] = grad_score.astype(jnp.bfloat16)
-            low_ref[rows, PAIR:] = probability.astype(jnp.bfloat16)
+        stat_ref[0:1] = inverse
+        stat_ref[1:2] = jnp.sum(delta, axis=0, keepdims=True) * inverse
 
     def gradients_stage(pair, buffer):
-        _, low_ref = buffer
+        both_ref, stat_ref = buffer
+        inverse, row_delta = stat_ref[0:1], stat_ref[1:2]
+        probability = both_ref[:, :PAIR] * inverse
+        score_low = (probability * (both_ref[:, PAIR:] - row_delta)).astype(jnp.bfloat16)
         grad_listed = lax.dot_general(
-            low_ref[...], diagonal_of(query_pair(pair)), NN, preferred_element_type=jnp.float32
+            jnp.concatenate([score_low, probability.astype(jnp.bfloat16)], axis=1),
+            diagonal_of(query_pair(pair)),
+            NN,
+            preferred_element_type=jnp.float32,
         )
         for n in range(NBR):
             for side in range(2):
@@ -155,9 +169,7 @@
                 acc_ref[pl.ds(start, BLOCK_TOK)] += grad_listed[
                     n * BLOCK_TOK : (n + 1) * BLOCK_TOK, side * PAIR : (side + 1) * PAIR
                 ]
-        grad_query = lax.dot_general(
-            low_ref[:, :PAIR], listed_keys(pair), TN, preferred_element_type=jnp.float32
-        )
+        grad_query = lax.dot_general(score_low, listed_keys(pair), TN, preferred_element_type=jnp.float32)
         low = lax.broadcasted_iota(jnp.int32, (BLOCK_TOK, PAIR), 1) < HEAD_DIM
         write_query(pair, jnp.where(low, grad_query[:BLOCK_TOK], grad_query[BLOCK_TOK:]) * SCALE)
 
@@ -227,7 +239,7 @@
 def work_buffers():
     return [
         pltpu.VMEM((LIST_ROWS, 2 * PAIR), jnp.float32),
-        pltpu.VMEM((LIST_ROWS, 2 * PAIR), jnp.bfloat16),
+        pltpu.VMEM((SUBLANES, PAIR), jnp.float32),
     ] * 2
 
 
@@ -266,10 +278,13 @@
         transcendentals=tokens * LIST_ROWS,
     )(start, place, packed.reshape(2 * tokens, PAIR))
     grads = lax.all_to_all(grads, axes, split_axis=0, concat_axis=0, tiled=True)
-    return call_kernel(
+    return pl.pallas_call(
         unpack_kernel,
-        (jax.ShapeDtypeStruct((rows, width), jnp.bfloat16),) * 3,
-        [in_vmem],
+        out_shape=(jax.ShapeDtypeStruct((rows, width), jnp.bfloat16),) * 3,
+        in_specs=[pl.BlockSpec(memory_space=in_vmem)],
+        out_specs=(pl.BlockSpec(memory_space=pl.ANY),) * 3,
+        scratch_shapes=[pltpu.VMEM((3, rows, width), jnp.bfloat16), pltpu.SemaphoreType.DMA((3,))],
+        compiler_params=pltpu.CompilerParams(vmem_limit_bytes=VMEM_LIMIT),
     )(grads)
 
 

time: 112 us -> 112 us (level)
  no operation moved by 1% of the time
where the time goes in v4:
time: 112 us
  blocking collectives  47.1 us (42%)
  waiting for transfers between devices  37.2 us (33%)
  Pallas kernels  14.9 us (13%)
  starting transfers between devices  7.46 us (7%)
  local copies, waits for them, and re-layouts  4.13 us (4%)
    all_to_all x1, blocking collectives, one_head_each(): grads = lax.all_to_all(grads, axes, split_axis=0, concat_axis=0, tiled=True)  47.1 us
    all_to_all x1, waiting for transfers between devices, one_head_each(): lax.all_to_all(packed, axes, split_axis=0, concat_axis=0, tiled=True)  37.2 us
    pallas_call x1, Pallas kernels, one_head_each(): call_kernel(head_kernel, jax.ShapeDtypeStruct((heads, 3 * rows // 2, PAIR...  10.6 us
    all_to_all x1, starting transfers between devices, one_head_each(): lax.all_to_all(packed, axes, split_axis=0, concat_axis=0, tiled=True)  7.46 us
    gather x2, local copies, waits for them, and re-layouts, listed_slots(): return block_slot[neighbours[sphere_of]]  3.95 us
    pallas_call x1, Pallas kernels, one_head_each(): pl.pallas_call(pack_kernel, grid=(2,), in_specs=[pl.BlockSpec((rows // 2,...  2.94 us
  transfers between devices with their start and end apart: 1, of which 1 were waited for; matrix products, arithmetic and copies ran while one was open for 4% of the time, Pallas kernels for 0%

profile of v4, /device:TPU:1, one launch (start us, length us, event | category | flops | bytes accessed | tf_op | source)
XLA Modules:
  0.0 111.6 jit_solution(9813761282700873205)
XLA Ops:
  0.6 2.9 %shard_map.85 = bf16[16,2,256,128]{3,2,1,0:T(8,128)(2,1)} custom-call(bf16[256,1024]{1,0:T(8,128)(2,1)} %query_ref.1, bf16[256,1024]{1,0:T(8,128)(2,1)} %grad_ref.1, bf16[256,1024]{1,0:T(8,128)(2,1)} %key_ref.1, bf16[256,1024]{1,0:T(8,128)(2,1)} %value_ref.1), custom_call_target="tpu_custom_call" | custom-call | tf_op jit(solution)/shard_map/pallas_call | solution.py:259
  3.6 0.0 copy-start.1
  3.6 0.0 copy-start
  3.6 7.5 %all-to-all-start = ((bf16[16,2,256,128]{3,2,1,0:T(8,128)(2,1)}), bf16[16,2,256,128]{3,2,1,0:T(8,128)(2,1)S(1)}, u32[]{:S(2)}, u32[]{:S(2)}) async-start(bf16[16,2,256,128]{3,2,1,0:T(8,128)(2,1)} %shard_map.85), calls=%async_computation | async-start | bytes 4194304 | tf_op jit(solution)/shard_map/all_to_all | solution.py:267
  11.0 0.0 copy-done.1
  11.0 0.1 copy.11
  11.1 0.0 copy-done
  11.1 0.1 select_reduce_fusion
  11.3 0.6 gather_fusion
  11.9 0.1 reshape.50
  12.0 3.3 %gather_fusion.1 = s32[512]{0:T(512)S(1)} fusion(s32[64]{0:T(128)S(1)} %copy-done, s32[1024]{0:T(1024)S(1)} %pad_clamp_fusion), kind=kCustom, calls=%fused_computation.1 | custom fusion | bytes 6144 | tf_op jit(solution)/shard_map/gather | solution.py:250
  15.3 37.2 %all-to-all-done = bf16[16,2,256,128]{3,2,1,0:T(8,128)(2,1)S(1)} async-done(((bf16[16,2,256,128]{3,2,1,0:T(8,128)(2,1)}), bf16[16,2,256,128]{3,2,1,0:T(8,128)(2,1)S(1)}, u32[]{:S(2)}, u32[]{:S(2)}) %all-to-all-start) | async-done | bytes 2097184 | tf_op jit(solution)/shard_map/all_to_all | solution.py:267
  52.5 10.6 %shard_map.86 = bf16[16,384,128]{2,1,0:T(8,128)(2,1)S(1)} custom-call(s32[512]{0:T(512)S(1)} %get-tuple-element.4.list_ref, s32[512]{0:T(512)S(1)} %get-tuple-element.3.place_ref, bf16[8192,128]{1,0:T(8,128)(2,1)S(1)} %bitcast.9), custom_call_target="tpu_custom_call" | custom-call | flops 1342177280 | bytes 3670016 | tf_op jit(solution)/shard_map/pallas_call | solution.py:270
  63.1 47.1 %all_to_all.10.packed_ref = bf16[16,384,128]{2,1,0:T(8,128)(2,1)S(1)} all-to-all(bf16[16,384,128]{2,1,0:T(8,128)(2,1)S(1)} %shard_map.86), channel_id=1, replica_groups=mesh['ctx'=4,'head'=4,'band'=2] {'ctx','head'}, dimensions={0} | all-to-all | bytes 3145728 | tf_op jit(solution)/shard_map/all_to_all | solution.py:280
  110.2 1.4 %shard_map.87 = (bf16[256,1024]{1,0:T(8,128)(2,1)}, bf16[256,1024]{1,0:T(8,128)(2,1)}, bf16[256,1024]{1,0:T(8,128)(2,1)}) custom-call(bf16[16,384,128]{2,1,0:T(8,128)(2,1)S(1)} %all_to_all.10.packed_ref), custom_call_target="tpu_custom_call" | custom-call | tf_op jit(solution)/shard_map/pallas_call | solution.py:281
  (5 shorter events, 0.0 us)
Async XLA Ops:
  3.6 7.5 %copy-start.1 = (s32[64,8]{0,1:T(8,128)S(1)}, s32[64,8]{0,1:T(8,128)}, u32[]{:S(2)}) copy-start(s32[64,8]{0,1:T(8,128)} %param.11) | copy-start | bytes 6148
  3.6 7.6 %copy-start = (s32[64]{0:T(128)S(1)}, s32[64]{0:T(128)}, u32[]{:S(2)}) copy-start(s32[64]{0:T(128)} %param.10) | copy-start | bytes 772
  3.6 48.9 %all-to-all-start = ((bf16[16,2,256,128]{3,2,1,0:T(8,128)(2,1)}), bf16[16,2,256,128]{3,2,1,0:T(8,128)(2,1)S(1)}, u32[]{:S(2)}, u32[]{:S(2)}) async-start(bf16[16,2,256,128]{3,2,1,0:T(8,128)(2,1)} %shard_map.85), calls=%async_computation | async-start | bytes 4194304 | tf_op jit(solution)/shard_map/all_to_all | solution.py:267

commit v5 on v4

--- a/solution.py
+++ b/solution.py
@@ -47,10 +47,31 @@
     return ref[:, head * HEAD_DIM : (head + 1) * HEAD_DIM]
 
 
-def pack_kernel(query_ref, grad_ref, key_ref, value_ref, out_ref):
-    for head in range(out_ref.shape[0]):
-        out_ref[head, 0] = jnp.concatenate([columns_of(query_ref, head), columns_of(grad_ref, head)], axis=1)
-        out_ref[head, 1] = jnp.concatenate([columns_of(key_ref, head), columns_of(value_ref, head)], axis=1)
+def pack_kernel(query_ref, grad_ref, key_ref, value_ref, out_ref, held, ready, in_sems, out_sems):
+    heads = out_ref.shape[0]
+    groups = out_sems.shape[1]
+    some = heads // groups
+    arrays = (query_ref, grad_ref, key_ref, value_ref)
+    loads = [pltpu.make_async_copy(array, held.at[n], in_sems.at[n]) for n, array in enumerate(arrays)]
+    for load in loads:
+        load.start()
+    stores = []
+    for kind in range(2):
+        left, right = 2 * kind, 2 * kind + 1
+        loads[left].wait()
+        loads[right].wait()
+        for group in range(groups):
+            for head in range(group * some, (group + 1) * some):
+                ready[head, kind] = jnp.concatenate(
+                    [columns_of(held.at[left], head), columns_of(held.at[right], head)], axis=1
+                )
+            part = pl.ds(group * some, some)
+            stores.append(
+                pltpu.make_async_copy(ready.at[part, kind], out_ref.at[part, kind], out_sems.at[kind, group])
+            )
+            stores[-1].start()
+    for store in stores:
+        store.wait()
 
 
 def unpack_kernel(packed_ref, query_ref, key_ref, value_ref, held, sems):
@@ -258,10 +279,15 @@
     in_vmem, in_smem = pltpu.VMEM, pltpu.SMEM
     packed = pl.pallas_call(
         pack_kernel,
-        grid=(2,),
-        in_specs=[pl.BlockSpec((rows // 2, width), lambda i: (i, 0))] * 4,
-        out_specs=pl.BlockSpec((heads, 2, rows // 2, PAIR), lambda i: (0, 0, i, 0)),
+        in_specs=[pl.BlockSpec(memory_space=pl.ANY)] * 4,
+        out_specs=pl.BlockSpec(memory_space=pl.ANY),
         out_shape=jax.ShapeDtypeStruct((heads, 2, rows, PAIR), jnp.bfloat16),
+        scratch_shapes=[
+            pltpu.VMEM((4, rows, width), jnp.bfloat16),
+            pltpu.VMEM((heads, 2, rows, PAIR), jnp.bfloat16),
+            pltpu.SemaphoreType.DMA((4,)),
+            pltpu.SemaphoreType.DMA((2, 2)),
+        ],
         compiler_params=pltpu.CompilerParams(vmem_limit_bytes=PACK_VMEM_LIMIT),
     )(queries, grad_output, key_states, value_states)
     packed = lax.all_to_all(packed, axes, split_axis=0, concat_axis=0, tiled=True)

time: 112 us -> 112 us (level)
  no operation moved by 1% of the time
where the time goes in v5:
time: 112 us; the launch traced here: 111 us
  blocking collectives  47.1 us (42%)
  waiting for transfers between devices  37.2 us (33%)
  Pallas kernels  14.8 us (13%)
  starting transfers between devices  7.33 us (7%)
  local copies, waits for them, and re-layouts  4.13 us (4%)
    all_to_all x1, blocking collectives, one_head_each(): grads = lax.all_to_all(grads, axes, split_axis=0, concat_axis=0, tiled=True)  47.1 us
    all_to_all x1, waiting for transfers between devices, one_head_each(): lax.all_to_all(packed, axes, split_axis=0, concat_axis=0, tiled=True)  37.2 us
    pallas_call x1, Pallas kernels, one_head_each(): call_kernel(head_kernel, jax.ShapeDtypeStruct((heads, 3 * rows // 2, PAIR...  10.6 us
    all_to_all x1, starting transfers between devices, one_head_each(): lax.all_to_all(packed, axes, split_axis=0, concat_axis=0, tiled=True)  7.33 us
    gather x2, local copies, waits for them, and re-layouts, listed_slots(): return block_slot[neighbours[sphere_of]]  3.95 us
    pallas_call x1, Pallas kernels, one_head_each(): pl.pallas_call(pack_kernel, in_specs=[pl.BlockSpec(memory_space=pl.ANY)]...  2.83 us
  transfers between devices with their start and end apart: 1, of which 1 were waited for; matrix products, arithmetic and copies ran while one was open for 4% of the time, Pallas kernels for 0%

profile of v5, /device:TPU:1, one launch (start us, length us, event | category | flops | bytes accessed | tf_op | source)
XLA Modules:
  0.0 111.4 jit_solution(8922256187025753770)
XLA Ops:
  0.6 2.8 %shard_map.85 = bf16[16,2,256,128]{3,2,1,0:T(8,128)(2,1)} custom-call(bf16[256,1024]{1,0:T(8,128)(2,1)} %query_ref.1, bf16[256,1024]{1,0:T(8,128)(2,1)} %grad_ref.1, bf16[256,1024]{1,0:T(8,128)(2,1)} %key_ref.1, bf16[256,1024]{1,0:T(8,128)(2,1)} %value_ref.1), custom_call_target="tpu_custom_call" | custom-call | tf_op jit(solution)/shard_map/pallas_call | solution.py:280
  3.5 0.0 copy-start.1
  3.5 0.0 copy-start
  3.5 7.3 %all-to-all-start = ((bf16[16,2,256,128]{3,2,1,0:T(8,128)(2,1)}), bf16[16,2,256,128]{3,2,1,0:T(8,128)(2,1)S(1)}, u32[]{:S(2)}, u32[]{:S(2)}) async-start(bf16[16,2,256,128]{3,2,1,0:T(8,128)(2,1)} %shard_map.85), calls=%async_computation | async-start | bytes 4194304 | tf_op jit(solution)/shard_map/all_to_all | solution.py:293
  10.8 0.0 copy-done.1
  10.8 0.1 copy.11
  10.9 0.0 copy-done
  10.9 0.1 select_reduce_fusion
  11.1 0.6 gather_fusion
  11.7 0.1 reshape.50
  11.8 3.3 %gather_fusion.1 = s32[512]{0:T(512)S(1)} fusion(s32[64]{0:T(128)S(1)} %copy-done, s32[1024]{0:T(1024)S(1)} %pad_clamp_fusion), kind=kCustom, calls=%fused_computation.1 | custom fusion | bytes 6144 | tf_op jit(solution)/shard_map/gather | solution.py:271
  15.1 37.2 %all-to-all-done = bf16[16,2,256,128]{3,2,1,0:T(8,128)(2,1)S(1)} async-done(((bf16[16,2,256,128]{3,2,1,0:T(8,128)(2,1)}), bf16[16,2,256,128]{3,2,1,0:T(8,128)(2,1)S(1)}, u32[]{:S(2)}, u32[]{:S(2)}) %all-to-all-start) | async-done | bytes 2097184 | tf_op jit(solution)/shard_map/all_to_all | solution.py:293
  52.3 10.6 %shard_map.86 = bf16[16,384,128]{2,1,0:T(8,128)(2,1)S(1)} custom-call(s32[512]{0:T(512)S(1)} %get-tuple-element.4.list_ref, s32[512]{0:T(512)S(1)} %get-tuple-element.3.place_ref, bf16[8192,128]{1,0:T(8,128)(2,1)S(1)} %bitcast.9), custom_call_target="tpu_custom_call" | custom-call | flops 1342177280 | bytes 3670016 | tf_op jit(solution)/shard_map/pallas_call | solution.py:296
  62.9 47.1 %all_to_all.10.packed_ref = bf16[16,384,128]{2,1,0:T(8,128)(2,1)S(1)} all-to-all(bf16[16,384,128]{2,1,0:T(8,128)(2,1)S(1)} %shard_map.86), channel_id=1, replica_groups=mesh['ctx'=4,'head'=4,'band'=2] {'ctx','head'}, dimensions={0} | all-to-all | bytes 3145728 | tf_op jit(solution)/shard_map/all_to_all | solution.py:306
  110.0 1.4 %shard_map.87 = (bf16[256,1024]{1,0:T(8,128)(2,1)}, bf16[256,1024]{1,0:T(8,128)(2,1)}, bf16[256,1024]{1,0:T(8,128)(2,1)}) custom-call(bf16[16,384,128]{2,1,0:T(8,128)(2,1)S(1)} %all_to_all.10.packed_ref), custom_call_target="tpu_custom_call" | custom-call | tf_op jit(solution)/shard_map/pallas_call | solution.py:307
  (5 shorter events, 0.0 us)
Async XLA Ops:
  3.5 7.4 %copy-start.1 = (s32[64,8]{0,1:T(8,128)S(1)}, s32[64,8]{0,1:T(8,128)}, u32[]{:S(2)}) copy-start(s32[64,8]{0,1:T(8,128)} %param.11) | copy-start | bytes 6148
  3.5 7.4 %copy-start = (s32[64]{0:T(128)S(1)}, s32[64]{0:T(128)}, u32[]{:S(2)}) copy-start(s32[64]{0:T(128)} %param.10) | copy-start | bytes 772
  3.5 48.8 %all-to-all-start = ((bf16[16,2,256,128]{3,2,1,0:T(8,128)(2,1)}), bf16[16,2,256,128]{3,2,1,0:T(8,128)(2,1)S(1)}, u32[]{:S(2)}, u32[]{:S(2)}) async-start(bf16[16,2,256,128]{3,2,1,0:T(8,128)(2,1)} %shard_map.85), calls=%async_computation | async-start | bytes 4194304 | tf_op jit(solution)/shard_map/all_to_all | solution.py:293

commit v6 on v4

--- a/solution.py
+++ b/solution.py
@@ -233,7 +233,7 @@
         out_ref[source, :rows] = (acc_ref[pl.ds(start, rows)] * key_scale()).astype(jnp.bfloat16)
         return carry
 
-    lax.fori_loop(0, sources, write, 0)
+    lax.fori_loop(0, sources, write, 0, unroll=4)
 
 
 def work_buffers():

time: 112 us -> 112 us (level)
  no operation moved by 1% of the time
where the time goes in v6:
time: 112 us
  blocking collectives  47.1 us (42%)
  waiting for transfers between devices  37.2 us (33%)
  Pallas kernels  14.9 us (13%)
  starting transfers between devices  7.46 us (7%)
  local copies, waits for them, and re-layouts  4.13 us (4%)
    all_to_all x1, blocking collectives, one_head_each(): grads = lax.all_to_all(grads, axes, split_axis=0, concat_axis=0, tiled=True)  47.1 us
    all_to_all x1, waiting for transfers between devices, one_head_each(): lax.all_to_all(packed, axes, split_axis=0, concat_axis=0, tiled=True)  37.2 us
    pallas_call x1, Pallas kernels, one_head_each(): call_kernel(head_kernel, jax.ShapeDtypeStruct((heads, 3 * rows // 2, PAIR...  10.6 us
    all_to_all x1, starting transfers between devices, one_head_each(): lax.all_to_all(packed, axes, split_axis=0, concat_axis=0, tiled=True)  7.46 us
    gather x2, local copies, waits for them, and re-layouts, listed_slots(): return block_slot[neighbours[sphere_of]]  3.95 us
    pallas_call x1, Pallas kernels, one_head_each(): pl.pallas_call(pack_kernel, grid=(2,), in_specs=[pl.BlockSpec((rows // 2,...  2.94 us
  transfers between devices with their start and end apart: 1, of which 1 were waited for; matrix products, arithmetic and copies ran while one was open for 4% of the time, Pallas kernels for 0%

profile of v6, /device:TPU:1, one launch (start us, length us, event | category | flops | bytes accessed | tf_op | source)
XLA Modules:
  0.0 111.6 jit_solution(6100654716725268662)
XLA Ops:
  0.6 2.9 %shard_map.85 = bf16[16,2,256,128]{3,2,1,0:T(8,128)(2,1)} custom-call(bf16[256,1024]{1,0:T(8,128)(2,1)} %query_ref.1, bf16[256,1024]{1,0:T(8,128)(2,1)} %grad_ref.1, bf16[256,1024]{1,0:T(8,128)(2,1)} %key_ref.1, bf16[256,1024]{1,0:T(8,128)(2,1)} %value_ref.1), custom_call_target="tpu_custom_call" | custom-call | tf_op jit(solution)/shard_map/pallas_call | solution.py:259
  3.6 0.0 copy-start.1
  3.6 0.0 copy-start
  3.6 7.5 %all-to-all-start = ((bf16[16,2,256,128]{3,2,1,0:T(8,128)(2,1)}), bf16[16,2,256,128]{3,2,1,0:T(8,128)(2,1)S(1)}, u32[]{:S(2)}, u32[]{:S(2)}) async-start(bf16[16,2,256,128]{3,2,1,0:T(8,128)(2,1)} %shard_map.85), calls=%async_computation | async-start | bytes 4194304 | tf_op jit(solution)/shard_map/all_to_all | solution.py:267
  11.0 0.0 copy-done.1
  11.0 0.1 copy.11
  11.1 0.0 copy-done
  11.1 0.1 select_reduce_fusion
  11.3 0.6 gather_fusion
  11.9 0.1 reshape.50
  12.0 3.3 %gather_fusion.1 = s32[512]{0:T(512)S(1)} fusion(s32[64]{0:T(128)S(1)} %copy-done, s32[1024]{0:T(1024)S(1)} %pad_clamp_fusion), kind=kCustom, calls=%fused_computation.1 | custom fusion | bytes 6144 | tf_op jit(solution)/shard_map/gather | solution.py:250
  15.3 37.2 %all-to-all-done = bf16[16,2,256,128]{3,2,1,0:T(8,128)(2,1)S(1)} async-done(((bf16[16,2,256,128]{3,2,1,0:T(8,128)(2,1)}), bf16[16,2,256,128]{3,2,1,0:T(8,128)(2,1)S(1)}, u32[]{:S(2)}, u32[]{:S(2)}) %all-to-all-start) | async-done | bytes 2097184 | tf_op jit(solution)/shard_map/all_to_all | solution.py:267
  52.5 10.6 %shard_map.86 = bf16[16,384,128]{2,1,0:T(8,128)(2,1)S(1)} custom-call(s32[512]{0:T(512)S(1)} %get-tuple-element.4.list_ref, s32[512]{0:T(512)S(1)} %get-tuple-element.3.place_ref, bf16[8192,128]{1,0:T(8,128)(2,1)S(1)} %bitcast.9), custom_call_target="tpu_custom_call" | custom-call | flops 1342177280 | bytes 3670016 | tf_op jit(solution)/shard_map/pallas_call | solution.py:270
  63.1 47.1 %all_to_all.10.packed_ref = bf16[16,384,128]{2,1,0:T(8,128)(2,1)S(1)} all-to-all(bf16[16,384,128]{2,1,0:T(8,128)(2,1)S(1)} %shard_map.86), channel_id=1, replica_groups=mesh['ctx'=4,'head'=4,'band'=2] {'ctx','head'}, dimensions={0} | all-to-all | bytes 3145728 | tf_op jit(solution)/shard_map/all_to_all | solution.py:280
  110.2 1.4 %shard_map.87 = (bf16[256,1024]{1,0:T(8,128)(2,1)}, bf16[256,1024]{1,0:T(8,128)(2,1)}, bf16[256,1024]{1,0:T(8,128)(2,1)}) custom-call(bf16[16,384,128]{2,1,0:T(8,128)(2,1)S(1)} %all_to_all.10.packed_ref), custom_call_target="tpu_custom_call" | custom-call | tf_op jit(solution)/shard_map/pallas_call | solution.py:281
  (5 shorter events, 0.0 us)
Async XLA Ops:
  3.6 7.5 %copy-start.1 = (s32[64,8]{0,1:T(8,128)S(1)}, s32[64,8]{0,1:T(8,128)}, u32[]{:S(2)}) copy-start(s32[64,8]{0,1:T(8,128)} %param.11) | copy-start | bytes 6148
  3.6 7.6 %copy-start = (s32[64]{0:T(128)S(1)}, s32[64]{0:T(128)}, u32[]{:S(2)}) copy-start(s32[64]{0:T(128)} %param.10) | copy-start | bytes 772
  3.6 48.9 %all-to-all-start = ((bf16[16,2,256,128]{3,2,1,0:T(8,128)(2,1)}), bf16[16,2,256,128]{3,2,1,0:T(8,128)(2,1)S(1)}, u32[]{:S(2)}, u32[]{:S(2)}) async-start(bf16[16,2,256,128]{3,2,1,0:T(8,128)(2,1)} %shard_map.85), calls=%async_computation | async-start | bytes 4194304 | tf_op jit(solution)/shard_map/all_to_all | solution.py:267

commit v7 on v5

--- a/solution.py
+++ b/solution.py
@@ -16,7 +16,7 @@
 SCALE = HEAD_DIM ** -0.5
 EXP2_SCALE = SCALE * math.log2(math.e)
 SUBLANES = 8
-CHUNK = 32
+CHUNK = 16
 VMEM_LIMIT = 48 * 1024 * 1024
 PACK_VMEM_LIMIT = 60 * 1024 * 1024
 NT = (((1,), (1,)), ((), ()))
@@ -254,7 +254,7 @@
         out_ref[source, :rows] = (acc_ref[pl.ds(start, rows)] * key_scale()).astype(jnp.bfloat16)
         return carry
 
-    lax.fori_loop(0, sources, write, 0)
+    lax.fori_loop(0, sources, write, 0, unroll=4)
 
 
 def work_buffers():

time: 112 us -> 112 us (level)
  no operation moved by 1% of the time
where the time goes in v7:
time: 112 us; the launch traced here: 111 us
  blocking collectives  47.1 us (42%)
  waiting for transfers between devices  37.2 us (33%)
  Pallas kernels  14.8 us (13%)
  starting transfers between devices  7.33 us (7%)
  local copies, waits for them, and re-layouts  4.13 us (4%)
    all_to_all x1, blocking collectives, one_head_each(): grads = lax.all_to_all(grads, axes, split_axis=0, concat_axis=0, tiled=True)  47.1 us
    all_to_all x1, waiting for transfers between devices, one_head_each(): lax.all_to_all(packed, axes, split_axis=0, concat_axis=0, tiled=True)  37.2 us
    pallas_call x1, Pallas kernels, one_head_each(): call_kernel(head_kernel, jax.ShapeDtypeStruct((heads, 3 * rows // 2, PAIR...  10.6 us
    all_to_all x1, starting transfers between devices, one_head_each(): lax.all_to_all(packed, axes, split_axis=0, concat_axis=0, tiled=True)  7.33 us
    gather x2, local copies, waits for them, and re-layouts, listed_slots(): return block_slot[neighbours[sphere_of]]  3.95 us
    pallas_call x1, Pallas kernels, one_head_each(): pl.pallas_call(pack_kernel, in_specs=[pl.BlockSpec(memory_space=pl.ANY)]...  2.83 us
  transfers between devices with their start and end apart: 1, of which 1 were waited for; matrix products, arithmetic and copies ran while one was open for 4% of the time, Pallas kernels for 0%

profile of v7, /device:TPU:1, one launch (start us, length us, event | category | flops | bytes accessed | tf_op | source)
XLA Modules:
  0.0 111.4 jit_solution(3729223207475124429)
XLA Ops:
  0.6 2.8 %shard_map.85 = bf16[16,2,256,128]{3,2,1,0:T(8,128)(2,1)} custom-call(bf16[256,1024]{1,0:T(8,128)(2,1)} %query_ref.1, bf16[256,1024]{1,0:T(8,128)(2,1)} %grad_ref.1, bf16[256,1024]{1,0:T(8,128)(2,1)} %key_ref.1, bf16[256,1024]{1,0:T(8,128)(2,1)} %value_ref.1), custom_call_target="tpu_custom_call" | custom-call | tf_op jit(solution)/shard_map/pallas_call | solution.py:280
  3.5 0.0 copy-start.1
  3.5 0.0 copy-start
  3.5 7.3 %all-to-all-start = ((bf16[16,2,256,128]{3,2,1,0:T(8,128)(2,1)}), bf16[16,2,256,128]{3,2,1,0:T(8,128)(2,1)S(1)}, u32[]{:S(2)}, u32[]{:S(2)}) async-start(bf16[16,2,256,128]{3,2,1,0:T(8,128)(2,1)} %shard_map.85), calls=%async_computation | async-start | bytes 4194304 | tf_op jit(solution)/shard_map/all_to_all | solution.py:293
  10.8 0.0 copy-done.1
  10.8 0.1 copy.11
  10.9 0.0 copy-done
  10.9 0.1 select_reduce_fusion
  11.1 0.6 gather_fusion
  11.7 0.1 reshape.50
  11.8 3.3 %gather_fusion.1 = s32[512]{0:T(512)S(1)} fusion(s32[64]{0:T(128)S(1)} %copy-done, s32[1024]{0:T(1024)S(1)} %pad_clamp_fusion), kind=kCustom, calls=%fused_computation.1 | custom fusion | bytes 6144 | tf_op jit(solution)/shard_map/gather | solution.py:271
  15.1 37.2 %all-to-all-done = bf16[16,2,256,128]{3,2,1,0:T(8,128)(2,1)S(1)} async-done(((bf16[16,2,256,128]{3,2,1,0:T(8,128)(2,1)}), bf16[16,2,256,128]{3,2,1,0:T(8,128)(2,1)S(1)}, u32[]{:S(2)}, u32[]{:S(2)}) %all-to-all-start) | async-done | bytes 2097184 | tf_op jit(solution)/shard_map/all_to_all | solution.py:293
  52.3 10.6 %shard_map.86 = bf16[16,384,128]{2,1,0:T(8,128)(2,1)S(1)} custom-call(s32[512]{0:T(512)S(1)} %get-tuple-element.4.list_ref, s32[512]{0:T(512)S(1)} %get-tuple-element.3.place_ref, bf16[8192,128]{1,0:T(8,128)(2,1)S(1)} %bitcast.9), custom_call_target="tpu_custom_call" | custom-call | flops 1342177280 | bytes 3670016 | tf_op jit(solution)/shard_map/pallas_call | solution.py:296
  62.9 47.1 %all_to_all.10.packed_ref = bf16[16,384,128]{2,1,0:T(8,128)(2,1)S(1)} all-to-all(bf16[16,384,128]{2,1,0:T(8,128)(2,1)S(1)} %shard_map.86), channel_id=1, replica_groups=mesh['ctx'=4,'head'=4,'band'=2] {'ctx','head'}, dimensions={0} | all-to-all | bytes 3145728 | tf_op jit(solution)/shard_map/all_to_all | solution.py:306
  110.0 1.4 %shard_map.87 = (bf16[256,1024]{1,0:T(8,128)(2,1)}, bf16[256,1024]{1,0:T(8,128)(2,1)}, bf16[256,1024]{1,0:T(8,128)(2,1)}) custom-call(bf16[16,384,128]{2,1,0:T(8,128)(2,1)S(1)} %all_to_all.10.packed_ref), custom_call_target="tpu_custom_call" | custom-call | tf_op jit(solution)/shard_map/pallas_call | solution.py:307
  (5 shorter events, 0.0 us)
Async XLA Ops:
  3.5 7.4 %copy-start.1 = (s32[64,8]{0,1:T(8,128)S(1)}, s32[64,8]{0,1:T(8,128)}, u32[]{:S(2)}) copy-start(s32[64,8]{0,1:T(8,128)} %param.11) | copy-start | bytes 6148
  3.5 7.4 %copy-start = (s32[64]{0:T(128)S(1)}, s32[64]{0:T(128)}, u32[]{:S(2)}) copy-start(s32[64]{0:T(128)} %param.10) | copy-start | bytes 772
  3.5 48.8 %all-to-all-start = ((bf16[16,2,256,128]{3,2,1,0:T(8,128)(2,1)}), bf16[16,2,256,128]{3,2,1,0:T(8,128)(2,1)S(1)}, u32[]{:S(2)}, u32[]{:S(2)}) async-start(bf16[16,2,256,128]{3,2,1,0:T(8,128)(2,1)} %shard_map.85), calls=%async_computation | async-start | bytes 4194304 | tf_op jit(solution)/shard_map/all_to_all | solution.py:293
